TPU v7x, 32 devices: a whole 2x2x4 slice. The times are simulated.
32 devices in a mesh: groups: 2 (over y), fsdp: 16 (over z, x, core).
Axes of the slice: x: 2, y: 2, z: 4, core: 2. Of those that a mesh axis runs over, the one named last changes fastest.
Arguments:
- inputs: bfloat16 [2048, 5120], P(('groups', 'fsdp')), parts along dimension 0, may hold values from -6 to 6
- out_grad: bfloat16 [2048, 5120], P(('groups', 'fsdp')), parts along dimension 0, may hold values from -6 to 6
- example_ids: int32 [2048], P(('groups', 'fsdp')), parts along dimension 0, may hold values from 0 to 1, never falling along the last dimension, each value on 1 to 768 neighbouring positions
- gate_weight: bfloat16 [5120, 13824], P(None, 'fsdp'), may hold values from -0.078125 to 0.078125
- up_weight: bfloat16 [5120, 13824], P(None, 'fsdp'), may hold values from -0.078125 to 0.078125
- down_weight: bfloat16 [13824, 5120], P('fsdp'), may hold values from -0.0546875 to 0.0546875
- unit_buckets: int32 [3, 13824], P(None, 'fsdp'), may hold values from 0 to 255
- unit_signs: int32 [3, 13824], P(None, 'fsdp'), may hold values from 0 to 1
- feature_buckets: int32 [5120], replicated, may hold values from 0 to 255
- feature_signs: int32 [5120], replicated, may hold values from 0 to 1
Outputs:
- sketch: float32 [4, 256, 256], P('groups', 'fsdp'), parts along dimension 0
There are 2 independent parts, one for each index of `groups`. A program takes and returns all parts, laid end to end along the dimension named above; an argument that names none is the same for every part. Nothing has to cross between parts.
Inputs may be any that keep to these rules, and one draw needn't show every extreme that they name: `example_ids`: ids never fall along the tokens; every example has 1 to min(1024, 768) tokens in one run.
All inputs are finite; a program needn't handle non-finite values.
Results may differ from a plain program's by a relative error of at most 0.0046.
Values may be sent and summed in bfloat16 or wider, within the bound.
No kernel may reach another device: no remote copies, remote signals or barrier semaphores. Data moves between devices by JAX's collectives and lax.ppermute only.
A program may use at most 128 MiB of HBM per device.

v0:
```python
import functools

import jax
import jax.numpy as jnp
from jax import lax
from jax.experimental import pallas as pl
from jax.experimental.pallas import tpu as pltpu
from jax.sharding import PartitionSpec as P

D = 5120
FF = 13824
EX = 2
SEQ = 512
K1 = 256
K2 = 256
CORES = 2
OUTER = 4
DEPTH = 2560
LANES = 128
VMEM_LIMIT = 12 << 20


def sign_tables(buckets, sign_bits, order):
    matches = buckets[..., None, :] == order[:, None]
    signed = (2 * sign_bits - 1).astype(jnp.bfloat16)[..., None, :]
    return jnp.where(matches, signed, jnp.zeros_like(signed))


class Layout:
    def __init__(self, count):
        self.outer = OUTER if count % (OUTER * CORES) == 0 else 1
        self.inner = count // (self.outer * CORES)
        self.count = count

    def index(self, outer, inner, core):
        return ((outer % self.outer) * self.inner + inner % self.inner) * CORES + core

    def pairs(self, step):
        places = [
            (o, i, c)
            for o in range(self.outer)
            for i in range(self.inner)
            for c in range(CORES)
        ]
        return [(self.index(o, i, c), self.index(*step(o, i, c))) for o, i, c in places]

    def outer_ring(self):
        return self.pairs(lambda o, i, c: (o + 1 - 2 * c, i, c))

    def inner_ring(self):
        return self.pairs(lambda o, i, c: (o, i + 1 - 2 * c, c))

    def core_swap(self):
        return self.pairs(lambda o, i, c: (o, i, 1 - c))


def dot(left, right):
    return jnp.dot(left, right, preferred_element_type=jnp.float32)


def dot_rows(left, right):
    return lax.dot_general(
        left, right, (((1,), (1,)), ((), ())), preferred_element_type=jnp.float32
    )


def joined(refs, lanes):
    parts = [ref[:, lanes] for ref in refs]
    return jnp.concatenate(parts, axis=0) if len(parts) > 1 else parts[0]


def add_products(refs, model, sums, depth):
    for acc, _ in sums:
        acc[...] = jnp.zeros_like(acc)

    def body(step, _):
        here = pl.ds(pl.multiple_of(step * depth, depth), depth)
        rows = joined(refs, here)
        for acc, weight in sums:
            acc[...] += dot_rows(rows, weight[:, here])
        return 0

    lax.fori_loop(0, model // depth, body, 0)


def forward_kernel(depth, pieces, *refs):
    gate_w, up_w, feature_w, tables = refs[pieces : pieces + 4]
    to_gate, to_up, down_part, feature_in = refs[pieces + 4 : pieces + 8]
    gate_acc, up_acc, feature_acc = refs[pieces + 8 :]
    sums = ((gate_acc, gate_w), (up_acc, up_w), (feature_acc, feature_w))
    add_products(refs[:pieces], gate_w.shape[1], sums, depth)
    gate, up = gate_acc[...], up_acc[...]
    sigmoid = jax.nn.sigmoid(gate)
    activated = gate * sigmoid
    to_gate[...] = up * sigmoid * (1.0 + gate * (1.0 - sigmoid))
    to_up[...] = activated
    hidden = (activated * up).astype(jnp.bfloat16)
    down_part[...] = dot_rows(hidden, tables[2]).astype(jnp.bfloat16)
    feature_in[...] = feature_acc[...].astype(jnp.bfloat16)


def backward_kernel(depth, pieces, *refs):
    down_w, feature_w, tables, to_gate, to_up, down_part, feature_in, before = refs[
        pieces : pieces + 8
    ]
    total, hidden_acc, feature_acc = refs[pieces + 8 :]
    model = down_w.shape[1]
    add_products(refs[:pieces], model, ((hidden_acc, down_w), (feature_acc, feature_w)), depth)
    bf16 = jnp.bfloat16
    hidden_grad = hidden_acc[...]
    gate_grad = (hidden_grad * to_gate[...]).astype(bf16)
    up_grad = (hidden_grad * to_up[...]).astype(bf16)
    input_part = (dot_rows(gate_grad, tables[0]) + dot_rows(up_grad, tables[1])).astype(bf16)
    example = joined(refs[:pieces], pl.ds(model, LANES)).astype(jnp.float32)
    example = jnp.concatenate([example] * (K2 // LANES), axis=1)

    def by_example(features):
        features = features.astype(jnp.float32)
        return jnp.concatenate(
            [jnp.where(example == e, features, 0.0) for e in range(EX)], axis=1
        ).astype(bf16)

    feature_out = feature_acc[...].astype(bf16)
    total[...] = before[...] + lax.dot_general(
        jnp.concatenate([down_part[...], input_part], axis=0),
        jnp.concatenate([by_example(feature_out), by_example(feature_in[...])], axis=0),
        (((0,), (0,)), ((), ())),
        preferred_element_type=jnp.float32,
    )


def on_chip(kernel, name, pieces, operands, outs, sums):
    rows = sum(piece.shape[0] for piece in pieces)
    vmem = pl.BlockSpec(memory_space=pltpu.VMEM)
    return pl.pallas_call(
        lambda *refs: kernel(len(pieces), *refs),
        in_specs=[vmem] * (len(pieces) + len(operands)),
        out_specs=[vmem] * len(outs),
        out_shape=outs,
        scratch_shapes=[pltpu.VMEM((rows, columns), jnp.float32) for columns in sums],
        compiler_params=pltpu.CompilerParams(vmem_limit_bytes=VMEM_LIMIT),
        cost_estimate=pl.CostEstimate(flops=0, bytes_accessed=0, transcendentals=0),
        name=name,
    )(*pieces, *operands)


def forward(pieces, gate_rows, up_rows, feature_table, tables, depth=DEPTH):
    units, model = gate_rows.shape
    kernel = functools.partial(forward_kernel, min(depth, model))
    rows = sum(piece.shape[0] for piece in pieces)
    outs = [
        jax.ShapeDtypeStruct((rows, units), jnp.float32),
        jax.ShapeDtypeStruct((rows, units), jnp.float32),
        jax.ShapeDtypeStruct((rows, K1), jnp.bfloat16),
        jax.ShapeDtypeStruct((rows, K2), jnp.bfloat16),
    ]
    operands = (gate_rows, up_rows, feature_table, tables)
    return on_chip(kernel, "forward", pieces, operands, outs, (units, units, K2))


def backward(pieces, down_rows, feature_table, tables, saved, before, depth=DEPTH):
    units, model = down_rows.shape
    kernel = functools.partial(backward_kernel, min(depth, model))
    outs = [jax.ShapeDtypeStruct(before.shape, jnp.float32)]
    operands = (down_rows, feature_table, tables, *saved, before)
    return on_chip(kernel, "backward", pieces, operands, outs, (units, K2))[0]


def on_device(
    layout,
    inputs,
    out_grad,
    example_ids,
    gate_weight,
    up_weight,
    down_weight,
    unit_buckets,
    unit_signs,
    feature_buckets,
    feature_signs,
):
    def move(value, pairs):
        return lax.ppermute(value, "fsdp", pairs)

    rows = inputs.shape[0]

    own_rows = K1 // layout.count
    order = jnp.arange(K1, dtype=jnp.int32).reshape(-1, CORES, own_rows).swapaxes(0, 1)
    order = jnp.where(lax.axis_index("fsdp") % CORES == 0, order, order[::-1]).reshape(-1)
    unit_tables = sign_tables(unit_buckets, unit_signs, order)
    feature_table = sign_tables(feature_buckets, feature_signs, jnp.arange(K2, dtype=jnp.int32))

    example = jnp.broadcast_to(example_ids[:, None], (rows, LANES)).astype(jnp.bfloat16)
    tagged = jnp.concatenate([out_grad, example], axis=1)
    gate_rows, up_rows = gate_weight.T, up_weight.T
    total = jnp.zeros((K1, EX * K2), jnp.float32)

    if layout.inner == 2 and layout.outer > 2:
        ahead = lambda piece: move(piece, layout.outer_ring())
        aside = lambda piece: move(piece, layout.inner_ring())
        swap = lambda piece, parts=2: [
            move(part, layout.core_swap()) for part in jnp.split(piece, parts, axis=0)
        ]
        after = lax.optimization_barrier
        first_side = lambda rows_in, *depth: forward(
            rows_in, gate_rows, up_rows, feature_table, unit_tables, *depth
        )
        other_side = lambda rows_out, saved, total, *depth: backward(
            rows_out, down_weight, feature_table, unit_tables, saved, total, *depth
        )
        width = inputs.shape[1]
        last = layout.outer - 1
        here_in, here_out = inputs, tagged
        coming_in = ahead(here_in), aside(here_in)
        here_out, feature_table, unit_tables = after((here_out, feature_table, unit_tables))
        coming_out = ahead(here_out), aside(here_out)
        swapped_in = swap(here_in)
        for step in range(1, last):
            next_in, across_in, total = after((*coming_in, total))
            coming_in = ahead(next_in), aside(next_in)
            swapped_across = swap(across_in)
            here_out, swapped_across = after((here_out, swapped_across))
            swapped_out = swap(here_out)
            saved = first_side([here_in, *swapped_in, across_in, *swapped_across])
            next_out, across_out, saved = after((*coming_out, saved))
            by_inner = aside(next_out) if step < last - 1 else ahead(across_out)
            coming_out = ahead(next_out), by_inner
            rows_out = [here_out, *swapped_out, across_out, *swap(across_out)]
            if step == last - 1:
                next_out, saved = after((next_out, saved))
                swapped_here, saved = after((swap(next_out), saved))
            total = other_side(rows_out, saved, total)
            here_in, total = after((next_in, total))
            here_out, swapped_in = next_out, swap(here_in)

        last_in, across_in, total = after((*coming_in, total))
        coming_in = aside(last_in)
        swapped_last, swapped_across = after((swap(last_in), swap(across_in)))
        saved = first_side([here_in, *swapped_in, last_in, *swapped_last])
        last_out, saved = after((coming_out[0], saved))
        coming_last = aside(last_out)
        rows_out = [here_out, *swapped_here, last_out, *swap(last_out)]
        total = other_side(rows_out, saved, total, width)
        corner_in = coming_in
        swapped_corner = swap(corner_in, 1)
        rows_in = [across_in, *swapped_across, corner_in, *swapped_corner]
        saved = first_side(rows_in, width)
        across_out, corner_out, total, saved = after((coming_out[1], coming_last, total, saved))
        swapped_out = swap(across_out)
        rows_out = [across_out, *swapped_out, corner_out, *swap(corner_out)]
        total = other_side(rows_out, saved, total, width)
    else:
        gather = lambda piece: lax.all_gather(piece, "fsdp", axis=0, tiled=True)
        saved = forward([gather(inputs)], gate_rows, up_rows, feature_table, unit_tables)
        total = backward([gather(tagged)], down_weight, feature_table, unit_tables, saved, total)

    half = K1 // CORES
    part = total[:half] + move(total[half:].astype(jnp.bfloat16), layout.core_swap())
    parts = part.astype(jnp.bfloat16).reshape(-1, own_rows, EX * K2)
    chips = [list(range(core, layout.count, CORES)) for core in range(CORES)]
    parts = lax.all_to_all(parts, "fsdp", 0, 0, axis_index_groups=chips)
    part = jnp.sum(parts.astype(jnp.float32), axis=0)
    factor = (3.0 * SEQ * FF * D / (K1 * K2)) ** (-0.5)
    return (factor * part).reshape(-1, EX, K2).transpose(1, 0, 2)


def solution(mesh):
    layout = Layout(mesh.shape["fsdp"])
    in_specs = (
        P(("groups", "fsdp"), None),
        P(("groups", "fsdp"), None),
        P(("groups", "fsdp")),
        P(None, "fsdp"),
        P(None, "fsdp"),
        P("fsdp", None),
        P(None, "fsdp"),
        P(None, "fsdp"),
        P(),
        P(),
    )
    out_specs = P("groups", "fsdp", None)
    return jax.shard_map(
        lambda *args: on_device(layout, *args),
        mesh=mesh,
        in_specs=in_specs,
        out_specs=out_specs,
        check_vma=False,
    )
```

profile of v0, /device:TPU:0, one launch (start us, length us, event | category | flops | bytes accessed | tf_op | source)
XLA Modules:
  0.0 130.8 jit_solution(353543155726515725)
XLA Ops:
  0.0 3.0 %collective-permute-start.4 = (bf16[64,5120]{1,0:T(8,128)(2,1)}, bf16[64,5120]{1,0:T(8,128)(2,1)S(1)}, u32[]{:S(2)}, u32[]{:S(2)}) collective-permute-start(bf16[64,5120]{1,0:T(8,128)(2,1)} %refs_0_.1), channel_id=1, source_target_pairs={{0,4},{1,13},{2,6},{3,15},{4,8},{5,1},{6,10},{7,3},{8,12},{9,5},{1... | collective-permute-start | bytes 1966088 | tf_op jit(solution)/shard_map/ppermute | solution.py:183
  3.0 1.5 %collective-permute-start.5 = (bf16[64,5120]{1,0:T(8,128)(2,1)}, bf16[64,5120]{1,0:T(8,128)(2,1)S(1)}, u32[]{:S(2)}, u32[]{:S(2)}) collective-permute-start(bf16[64,5120]{1,0:T(8,128)(2,1)} %refs_0_.1), channel_id=1, source_target_pairs={{0,2},{1,3},{2,0},{3,1},{4,6},{5,7},{6,4},{7,5},{8,10},{9,11},{10,... | collective-permute-start | bytes 1966088 | tf_op jit(solution)/shard_map/ppermute | solution.py:183
  4.5 0.7 convert_element_type.20
  5.2 0.7 add_convert_fusion
  6.0 0.7 add_convert_fusion.1
  6.7 1.4 %fusion.refs_8_.refs_7_ = bf16[256,5120]{1,0:T(8,128)(2,1)S(1)} fusion(s32[5120]{0:T(1024)} %param.18, bf16[5120]{0:T(1024)(128)(2,1)S(1)} %add_convert_fusion), kind=kLoop, calls=%fused_computation.1 | loop fusion | flops 2621440 | bytes 2652160 | tf_op jit(solution)/shard_map/jit(_where)/select_n | solution.py:26
  8.2 0.4 compare_select_fusion.refs_9_.refs_8_
  8.8 1.6 %collective-permute-start = (bf16[64,5248]{1,0:T(8,128)(2,1)S(1)}, bf16[64,5248]{1,0:T(8,128)(2,1)S(1)}, u32[]{:S(2)}, u32[]{:S(2)}) collective-permute-start(bf16[64,5248]{1,0:T(8,128)(2,1)S(1)} %pad_maximum_fusion.refs_0_), channel_id=1, source_target_pairs={{0,4},{1,13},{2,6},{3,15},{4,8},{5,1},{6,10},{7,3},{8,12},{9,5},{1... | collective-permute-start | bytes 2015240 | tf_op jit(solution)/shard_map/ppermute | solution.py:183
  10.4 0.5 collective-permute-start.1
  11.0 9.8 %collective-permute-done.4.refs_0_ = bf16[64,5120]{1,0:T(8,128)(2,1)S(1)} collective-permute-done((bf16[64,5120]{1,0:T(8,128)(2,1)}, bf16[64,5120]{1,0:T(8,128)(2,1)S(1)}, u32[]{:S(2)}, u32[]{:S(2)}) %collective-permute-start.4) | collective-permute-done | bytes 655392 | tf_op jit(solution)/shard_map/ppermute | solution.py:183
  20.9 0.8 collective-permute-start.6
  21.8 0.5 collective-permute-start.2
  22.3 0.6 collective-permute-done.6.refs_4_
  22.9 0.4 collective-permute-start.3
  23.4 1.3 %collective-permute-start.16 = (bf16[64,5120]{1,0:T(8,128)(2,1)S(1)}, bf16[64,5120]{1,0:T(8,128)(2,1)S(1)}, u32[]{:S(2)}, u32[]{:S(2)}) collective-permute-start(bf16[64,5120]{1,0:T(8,128)(2,1)S(1)} %collective-permute-done.4.refs_0_), channel_id=1, source_target_pairs={{0,4},{1,13},{2,6},{3,15},{4,8},{5,1},{6,10},{7,3},{8,12},{9,5},{1... | collective-permute-start | bytes 1966088 | tf_op jit(solution)/shard_map/ppermute | solution.py:183
  24.7 1.5 %collective-permute-start.17 = (bf16[64,5120]{1,0:T(8,128)(2,1)S(1)}, bf16[64,5120]{1,0:T(8,128)(2,1)S(1)}, u32[]{:S(2)}, u32[]{:S(2)}) collective-permute-start(bf16[64,5120]{1,0:T(8,128)(2,1)S(1)} %collective-permute-done.4.refs_0_), channel_id=1, source_target_pairs={{0,2},{1,3},{2,0},{3,1},{4,6},{5,7},{6,4},{7,5},{8,10},{9,11},{10,... | collective-permute-start | bytes 1966088 | tf_op jit(solution)/shard_map/ppermute | solution.py:183
  26.2 3.5 %copy-done = bf16[5120,864]{0,1:T(8,128)(2,1)S(1)} copy-done((bf16[5120,864]{0,1:T(8,128)(2,1)S(1)}, bf16[5120,864]{0,1:T(8,128)(2,1)}, u32[]{:S(2)}) %copy-start) | copy-done | bytes 8847384
  29.7 3.5 %copy-done.1 = bf16[5120,864]{0,1:T(8,128)(2,1)S(1)} copy-done((bf16[5120,864]{0,1:T(8,128)(2,1)S(1)}, bf16[5120,864]{0,1:T(8,128)(2,1)}, u32[]{:S(2)}) %copy-start.1) | copy-done | bytes 8847384
  33.2 7.2 %forward.4 = (f32[256,864]{1,0:T(8,128)S(1)}, f32[256,864]{1,0:T(8,128)S(1)}, bf16[256,256]{1,0:T(8,128)(2,1)S(1)}, bf16[256,256]{1,0:T(8,128)(2,1)S(1)}) custom-call(bf16[64,5120]{1,0:T(8,128)(2,1)S(1)} %copy-done.3, bf16[32,5120]{1,0:T(8,128)(2,1)S(1)} %collective-permute-done.2.refs_1_, bf16[32,5120]{1,0:T(8,128)(2,1)S(1)} %collective-permute-done.3.refs_2_, ...), custom_call_target="tpu_custom_call" | custom-call | tf_op jit(solution)/shard_map/forward/pallas_call | solution.py:135
  40.5 0.4 collective-permute-start.10
  41.1 0.4 collective-permute-start.12
  41.5 0.7 collective-permute-done.10.refs_1_
  42.7 1.6 %collective-permute-start.8 = (bf16[64,5248]{1,0:T(8,128)(2,1)S(1)}, bf16[64,5248]{1,0:T(8,128)(2,1)S(1)}, u32[]{:S(2)}, u32[]{:S(2)}) collective-permute-start(bf16[64,5248]{1,0:T(8,128)(2,1)S(1)} %collective-permute-done.refs_0_), channel_id=1, source_target_pairs={{0,4},{1,13},{2,6},{3,15},{4,8},{5,1},{6,10},{7,3},{8,12},{9,5},{1... | collective-permute-start | bytes 2015240 | tf_op jit(solution)/shard_map/ppermute | solution.py:183
  44.3 0.5 collective-permute-start.9
  44.9 3.7 %copy-done.2 = bf16[864,5120]{1,0:T(8,128)(2,1)S(1)} copy-done((bf16[864,5120]{1,0:T(8,128)(2,1)S(1)}, bf16[864,5120]{1,0:T(8,128)(2,1)}, u32[]{:S(2)}) %copy-start.2) | copy-done | bytes 8847384
  48.5 4.8 %backward.4.refs_13_ = f32[256,512]{1,0:T(8,128)S(1)} custom-call(bf16[64,5248]{1,0:T(8,128)(2,1)S(1)} %pad_maximum_fusion.refs_0_, bf16[32,5248]{1,0:T(8,128)(2,1)S(1)} %collective-permute-done.10.refs_1_, bf16[32,5248]{1,0:T(8,128)(2,1)S(1)} %collective-permute-done.11.refs_2_, bf16[64,5248]{1,0:T(8,128)(2,1)S(1)} %collective-permute-done.1.refs_3_, ...), custom_call_target="tpu_custom_call" | custom-call | tf_op jit(solution)/shard_map/backward/pallas_call | solution.py:135
  53.4 0.6 collective-permute-start.18
  54.1 0.5 collective-permute-start.14
  54.6 0.6 collective-permute-done.18.refs_4_
  55.2 0.4 collective-permute-start.15
  55.7 0.5 collective-permute-start.30
  56.3 1.4 %collective-permute-start.31 = (bf16[64,5120]{1,0:T(8,128)(2,1)S(1)}, bf16[64,5120]{1,0:T(8,128)(2,1)S(1)}, u32[]{:S(2)}, u32[]{:S(2)}) collective-permute-start(bf16[64,5120]{1,0:T(8,128)(2,1)S(1)} %collective-permute-done.16.refs_0_), channel_id=1, source_target_pairs={{0,2},{1,3},{2,0},{3,1},{4,6},{5,7},{6,4},{7,5},{8,10},{9,11},{10,... | collective-permute-start | bytes 1966088 | tf_op jit(solution)/shard_map/ppermute | solution.py:183
  57.7 1.4 %collective-permute-start.22 = (bf16[32,5248]{1,0:T(8,128)(2,1)S(1)}, bf16[32,5248]{1,0:T(8,128)(2,1)S(1)}, u32[]{:S(2)}, u32[]{:S(2)}) collective-permute-start(bf16[32,5248]{1,0:T(8,128)(2,1)S(1)} %get-tuple-element.170), channel_id=1, source_target_pairs={{0,1},{1,0},{2,3},{3,2},{4,5},{5,4},{6,7},{7,6},{8,9},{9,8},{10,11... | collective-permute-start | bytes 1007624 | tf_op jit(solution)/shard_map/ppermute | solution.py:183
  59.2 7.2 %forward.5 = (f32[256,864]{1,0:T(8,128)S(1)}, f32[256,864]{1,0:T(8,128)S(1)}, bf16[256,256]{1,0:T(8,128)(2,1)S(1)}, bf16[256,256]{1,0:T(8,128)(2,1)S(1)}) custom-call(bf16[64,5120]{1,0:T(8,128)(2,1)S(1)} %collective-permute-done.4.refs_0_, bf16[32,5120]{1,0:T(8,128)(2,1)S(1)} %collective-permute-done.14.refs_1_, ...), custom_call_target="tpu_custom_call" | custom-call | tf_op jit(solution)/shard_map/forward/pallas_call | solution.py:135
  66.5 0.5 collective-permute-start.27
  67.2 0.9 collective-permute-done.26.refs_1_
  69.8 0.5 collective-permute-done.25.refs_5_
  70.3 4.9 %backward.5.refs_13_ = f32[256,512]{1,0:T(8,128)S(1)} custom-call(bf16[64,5248]{1,0:T(8,128)(2,1)S(1)} %collective-permute-done.refs_0_, bf16[32,5248]{1,0:T(8,128)(2,1)S(1)} %collective-permute-done.22.refs_1_, bf16[32,5248]{1,0:T(8,128)(2,1)S(1)} %collective-permute-done.23.refs_2_, bf16[64,5248]{1,0:T(8,128)(2,1)S(1)} %collective-permute-done.9.refs_3_, ...), custom_call_target="tpu_custom_call" | custom-call | tf_op jit(solution)/shard_map/backward/pallas_call | solution.py:135
  75.2 2.5 %collective-permute-done.30.refs_3_ = bf16[64,5120]{1,0:T(8,128)(2,1)S(1)} collective-permute-done((bf16[64,5120]{1,0:T(8,128)(2,1)S(1)}, bf16[64,5120]{1,0:T(8,128)(2,1)S(1)}, u32[]{:S(2)}, u32[]{:S(2)}) %collective-permute-start.30) | collective-permute-done | bytes 655392 | tf_op jit(solution)/shard_map/ppermute | solution.py:183
  77.7 1.8 %collective-permute-start.39 = (bf16[64,5120]{1,0:T(8,128)(2,1)S(1)}, bf16[64,5120]{1,0:T(8,128)(2,1)S(1)}, u32[]{:S(2)}, u32[]{:S(2)}) collective-permute-start(bf16[64,5120]{1,0:T(8,128)(2,1)S(1)} %collective-permute-done.30.refs_3_), channel_id=1, source_target_pairs={{0,2},{1,3},{2,0},{3,1},{4,6},{5,7},{6,4},{7,5},{8,10},{9,11},{10,... | collective-permute-start | bytes 1966088 | tf_op jit(solution)/shard_map/ppermute | solution.py:183
  79.5 0.5 collective-permute-start.33
  80.2 0.9 collective-permute-done.32.refs_4_
  82.2 0.6 collective-permute-done.35.refs_2_
  82.8 0.5 collective-permute-done.28.refs_1_
  83.3 0.5 collective-permute-done.29.refs_2_
  83.7 7.4 %forward.6 = (f32[256,864]{1,0:T(8,128)S(1)}, f32[256,864]{1,0:T(8,128)S(1)}, bf16[256,256]{1,0:T(8,128)(2,1)S(1)}, bf16[256,256]{1,0:T(8,128)(2,1)S(1)}) custom-call(bf16[64,5120]{1,0:T(8,128)(2,1)S(1)} %collective-permute-done.16.refs_0_, bf16[32,5120]{1,0:T(8,128)(2,1)S(1)} %collective-permute-done.28.refs_1_, ...), custom_call_target="tpu_custom_call" | custom-call | tf_op jit(solution)/shard_map/forward/pallas_call | solution.py:135
  91.1 1.0 collective-permute-done.21.refs_3_
  92.1 1.7 %collective-permute-start.36 = (bf16[64,5248]{1,0:T(8,128)(2,1)S(1)}, bf16[64,5248]{1,0:T(8,128)(2,1)S(1)}, u32[]{:S(2)}, u32[]{:S(2)}) collective-permute-start(bf16[64,5248]{1,0:T(8,128)(2,1)S(1)} %collective-permute-done.21.refs_3_), channel_id=1, source_target_pairs={{0,2},{1,3},{2,0},{3,1},{4,6},{5,7},{6,4},{7,5},{8,10},{9,11},{10,... | collective-permute-start | bytes 2015240 | tf_op jit(solution)/shard_map/ppermute | solution.py:183
  93.8 0.8 collective-permute-done.39.refs_3_
  94.6 0.6 collective-permute-start.37
  95.3 1.9 %collective-permute-done.37.refs_4_ = bf16[32,5248]{1,0:T(8,128)(2,1)S(1)} collective-permute-done((bf16[32,5248]{1,0:T(8,128)(2,1)S(1)}, bf16[32,5248]{1,0:T(8,128)(2,1)S(1)}, u32[]{:S(2)}, u32[]{:S(2)}) %collective-permute-start.37) | collective-permute-done | bytes 335904 | tf_op jit(solution)/shard_map/ppermute | solution.py:183
  97.2 0.5 collective-permute-done.38.refs_5_
  97.7 4.5 %backward.6.refs_13_ = f32[256,512]{1,0:T(8,128)S(1)} custom-call(bf16[64,5248]{1,0:T(8,128)(2,1)S(1)} %collective-permute-done.8.refs_0_, bf16[32,5248]{1,0:T(8,128)(2,1)S(1)} %collective-permute-done.26.refs_1_, bf16[32,5248]{1,0:T(8,128)(2,1)S(1)} %collective-permute-done.27.refs_2_, bf16[64,5248]{1,0:T(8,128)(2,1)S(1)} %collective-permute-done.21.refs_3_, ...), custom_call_target="tpu_custom_call" | custom-call | tf_op jit(solution)/shard_map/backward/pallas_call | solution.py:135
  102.2 6.7 %forward.7 = (f32[256,864]{1,0:T(8,128)S(1)}, f32[256,864]{1,0:T(8,128)S(1)}, bf16[256,256]{1,0:T(8,128)(2,1)S(1)}, bf16[256,256]{1,0:T(8,128)(2,1)S(1)}) custom-call(bf16[64,5120]{1,0:T(8,128)(2,1)S(1)} %collective-permute-done.31.refs_0_, bf16[32,5120]{1,0:T(8,128)(2,1)S(1)} %collective-permute-done.34.refs_1_, ...), custom_call_target="tpu_custom_call" | custom-call | tf_op jit(solution)/shard_map/forward/pallas_call | solution.py:135
  109.1 0.5 collective-permute-start.42
  109.8 0.4 collective-permute-start.44
  110.3 0.5 collective-permute-done.41.refs_1_
  110.8 0.5 collective-permute-done.42.refs_2_
  111.2 0.5 collective-permute-done.43.refs_4_
  111.7 0.5 collective-permute-done.44.refs_5_
  112.2 4.8 %backward.7 = f32[256,512]{1,0:T(8,128)S(1)} custom-call(bf16[64,5248]{1,0:T(8,128)(2,1)S(1)} %collective-permute-done.20.refs_0_, bf16[32,5248]{1,0:T(8,128)(2,1)S(1)} %collective-permute-done.41.refs_1_, bf16[32,5248]{1,0:T(8,128)(2,1)S(1)} %collective-permute-done.42.refs_2_, bf16[64,5248]{1,0:T(8,128)(2,1)S(1)} %collective-permute-done.36.refs_3_, ...), custom_call_target="tpu_custom_call" | custom-call | tf_op jit(solution)/shard_map/backward/pallas_call | solution.py:135
  117.2 1.2 collective-permute-done.45
  118.5 11.6 %all_to_all.5 = bf16[8,16,512]{2,1,0:T(8,128)(2,1)S(1)} all-to-all(bf16[8,16,512]{2,1,0:T(8,128)(2,1)S(1)} %bitcast.18), channel_id=1, replica_groups={{0,2,4,6,8,10,12,14},{1,3,5,7,9,11,13,15},{16,18,20,22,24,26,28,30},{17..., dimensions={0} | all-to-all | bytes 262144 | tf_op jit(solution)/shard_map/all_to_all | solution.py:261
  130.2 0.6 copy.11
  (102 shorter events, 5.9 us)
Async XLA Ops:
  0.0 8.2 %copy-start.5 = (s32[3,864]{1,0:T(4,128)S(1)}, s32[3,864]{1,0:T(4,128)}, u32[]{:S(2)}) copy-start(s32[3,864]{1,0:T(4,128)} %param.16) | copy-start | bytes 31108
  0.0 8.7 %copy-start.4 = (bf16[64,5120]{1,0:T(8,128)(2,1)S(1)}, bf16[64,5120]{1,0:T(8,128)(2,1)}, u32[]{:S(2)}) copy-start(bf16[64,5120]{1,0:T(8,128)(2,1)} %param.11) | copy-start | bytes 1966084
  0.0 20.8 %collective-permute-start.4 = (bf16[64,5120]{1,0:T(8,128)(2,1)}, bf16[64,5120]{1,0:T(8,128)(2,1)S(1)}, u32[]{:S(2)}, u32[]{:S(2)}) collective-permute-start(bf16[64,5120]{1,0:T(8,128)(2,1)} %refs_0_.1), channel_id=1, source_target_pairs={{0,4},{1,13},{2,6},{3,15},{4,8},{5,1},{6,10},{7,3},{8,12},{9,5},{1... | collective-permute-start | bytes 1966088 | tf_op jit(solution)/shard_map/ppermute | solution.py:183
  3.0 17.8 %collective-permute-start.5 = (bf16[64,5120]{1,0:T(8,128)(2,1)}, bf16[64,5120]{1,0:T(8,128)(2,1)S(1)}, u32[]{:S(2)}, u32[]{:S(2)}) collective-permute-start(bf16[64,5120]{1,0:T(8,128)(2,1)} %refs_0_.1), channel_id=1, source_target_pairs={{0,2},{1,3},{2,0},{3,1},{4,6},{5,7},{6,4},{7,5},{8,10},{9,11},{10,... | collective-permute-start | bytes 1966088 | tf_op jit(solution)/shard_map/ppermute | solution.py:183
  8.2 13.5 %copy-start.3 = (bf16[64,5120]{1,0:T(8,128)(2,1)S(1)}, bf16[64,5120]{1,0:T(8,128)(2,1)}, u32[]{:S(2)}) copy-start(bf16[64,5120]{1,0:T(8,128)(2,1)} %refs_0_.1) | copy-start | bytes 1966084
  8.8 31.6 %collective-permute-start = (bf16[64,5248]{1,0:T(8,128)(2,1)S(1)}, bf16[64,5248]{1,0:T(8,128)(2,1)S(1)}, u32[]{:S(2)}, u32[]{:S(2)}) collective-permute-start(bf16[64,5248]{1,0:T(8,128)(2,1)S(1)} %pad_maximum_fusion.refs_0_), channel_id=1, source_target_pairs={{0,4},{1,13},{2,6},{3,15},{4,8},{5,1},{6,10},{7,3},{8,12},{9,5},{1... | collective-permute-start | bytes 2015240 | tf_op jit(solution)/shard_map/ppermute | solution.py:183
  10.4 30.0 %collective-permute-start.1 = (bf16[64,5248]{1,0:T(8,128)(2,1)S(1)}, bf16[64,5248]{1,0:T(8,128)(2,1)S(1)}, u32[]{:S(2)}, u32[]{:S(2)}) collective-permute-start(bf16[64,5248]{1,0:T(8,128)(2,1)S(1)} %pad_maximum_fusion.refs_0_), channel_id=1, source_target_pairs={{0,2},{1,3},{2,0},{3,1},{4,6},{5,7},{6,4},{7,5},{8,10},{9,11},{10,... | collective-permute-start | bytes 2015240 | tf_op jit(solution)/shard_map/ppermute | solution.py:183
  20.9 2.0 %collective-permute-start.6 = (bf16[32,5120]{1,0:T(8,128)(2,1)S(1)}, bf16[32,5120]{1,0:T(8,128)(2,1)S(1)}, u32[]{:S(2)}, u32[]{:S(2)}) collective-permute-start(bf16[32,5120]{1,0:T(8,128)(2,1)S(1)} %get-tuple-element.186), channel_id=1, source_target_pairs={{0,1},{1,0},{2,3},{3,2},{4,5},{5,4},{6,7},{7,6},{8,9},{9,8},{10,11... | collective-permute-start | bytes 983048 | tf_op jit(solution)/shard_map/ppermute | solution.py:183
  21.6 1.7 %collective-permute-start.7 = (bf16[32,5120]{1,0:T(8,128)(2,1)S(1)}, bf16[32,5120]{1,0:T(8,128)(2,1)S(1)}, u32[]{:S(2)}, u32[]{:S(2)}) collective-permute-start(bf16[32,5120]{1,0:T(8,128)(2,1)S(1)} %get-tuple-element.185), channel_id=1, source_target_pairs={{0,1},{1,0},{2,3},{3,2},{4,5},{5,4},{6,7},{7,6},{8,9},{9,8},{10,11... | collective-permute-start | bytes 983048 | tf_op jit(solution)/shard_map/ppermute | solution.py:183
  21.8 2.9 %collective-permute-start.2 = (bf16[32,5120]{1,0:T(8,128)(2,1)S(1)}, bf16[32,5120]{1,0:T(8,128)(2,1)S(1)}, u32[]{:S(2)}, u32[]{:S(2)}) collective-permute-start(bf16[32,5120]{1,0:T(8,128)(2,1)S(1)} %get-tuple-element.188), channel_id=1, source_target_pairs={{0,1},{1,0},{2,3},{3,2},{4,5},{5,4},{6,7},{7,6},{8,9},{9,8},{10,11... | collective-permute-start | bytes 983048 | tf_op jit(solution)/shard_map/ppermute | solution.py:183
  22.9 3.3 %collective-permute-start.3 = (bf16[32,5120]{1,0:T(8,128)(2,1)S(1)}, bf16[32,5120]{1,0:T(8,128)(2,1)S(1)}, u32[]{:S(2)}, u32[]{:S(2)}) collective-permute-start(bf16[32,5120]{1,0:T(8,128)(2,1)S(1)} %get-tuple-element.187), channel_id=1, source_target_pairs={{0,1},{1,0},{2,3},{3,2},{4,5},{5,4},{6,7},{7,6},{8,9},{9,8},{10,11... | collective-permute-start | bytes 983048 | tf_op jit(solution)/shard_map/ppermute | solution.py:183
  23.4 30.0 %collective-permute-start.16 = (bf16[64,5120]{1,0:T(8,128)(2,1)S(1)}, bf16[64,5120]{1,0:T(8,128)(2,1)S(1)}, u32[]{:S(2)}, u32[]{:S(2)}) collective-permute-start(bf16[64,5120]{1,0:T(8,128)(2,1)S(1)} %collective-permute-done.4.refs_0_), channel_id=1, source_target_pairs={{0,4},{1,13},{2,6},{3,15},{4,8},{5,1},{6,10},{7,3},{8,12},{9,5},{1... | collective-permute-start | bytes 1966088 | tf_op jit(solution)/shard_map/ppermute | solution.py:183
  24.7 28.7 %collective-permute-start.17 = (bf16[64,5120]{1,0:T(8,128)(2,1)S(1)}, bf16[64,5120]{1,0:T(8,128)(2,1)S(1)}, u32[]{:S(2)}, u32[]{:S(2)}) collective-permute-start(bf16[64,5120]{1,0:T(8,128)(2,1)S(1)} %collective-permute-done.4.refs_0_), channel_id=1, source_target_pairs={{0,2},{1,3},{2,0},{3,1},{4,6},{5,7},{6,4},{7,5},{8,10},{9,11},{10,... | collective-permute-start | bytes 1966088 | tf_op jit(solution)/shard_map/ppermute | solution.py:183
  26.2 3.5 %copy-start = (bf16[5120,864]{0,1:T(8,128)(2,1)S(1)}, bf16[5120,864]{0,1:T(8,128)(2,1)}, u32[]{:S(2)}) copy-start(bf16[5120,864]{0,1:T(8,128)(2,1)} %param.13) | copy-start | bytes 26542084
  29.7 3.5 %copy-start.1 = (bf16[5120,864]{0,1:T(8,128)(2,1)S(1)}, bf16[5120,864]{0,1:T(8,128)(2,1)}, u32[]{:S(2)}) copy-start(bf16[5120,864]{0,1:T(8,128)(2,1)} %param.14) | copy-start | bytes 26542084
  33.2 25.9 %slice-start.3 = ((s8[8847360]{0:T(1024)(128)(4,1)}), s8[4194304]{0:T(1024)(128)(4,1)S(1)}, s32[]{:S(2)}) async-start(s8[8847360]{0:T(1024)(128)(4,1)} %bitcast.11), calls=%async_computation.4 | async-start | bytes 8388608
  33.2 25.9 %slice-start.4 = ((s8[8847360]{0:T(1024)(128)(4,1)}), s8[4194304]{0:T(1024)(128)(4,1)S(1)}, s32[]{:S(2)}) async-start(s8[8847360]{0:T(1024)(128)(4,1)} %bitcast.11), calls=%async_computation.5 | async-start | bytes 8388608
  40.5 1.7 %collective-permute-start.10 = (bf16[32,5248]{1,0:T(8,128)(2,1)S(1)}, bf16[32,5248]{1,0:T(8,128)(2,1)S(1)}, u32[]{:S(2)}, u32[]{:S(2)}) collective-permute-start(bf16[32,5248]{1,0:T(8,128)(2,1)S(1)} %get-tuple-element.174), channel_id=1, source_target_pairs={{0,1},{1,0},{2,3},{3,2},{4,5},{5,4},{6,7},{7,6},{8,9},{9,8},{10,11... | collective-permute-start | bytes 1007624 | tf_op jit(solution)/shard_map/ppermute | solution.py:183
  40.9 1.8 %collective-permute-start.11 = (bf16[32,5248]{1,0:T(8,128)(2,1)S(1)}, bf16[32,5248]{1,0:T(8,128)(2,1)S(1)}, u32[]{:S(2)}, u32[]{:S(2)}) collective-permute-start(bf16[32,5248]{1,0:T(8,128)(2,1)S(1)} %get-tuple-element.173), channel_id=1, source_target_pairs={{0,1},{1,0},{2,3},{3,2},{4,5},{5,4},{6,7},{7,6},{8,9},{9,8},{10,11... | collective-permute-start | bytes 1007624 | tf_op jit(solution)/shard_map/ppermute | solution.py:183
  41.1 3.1 %collective-permute-start.12 = (bf16[32,5248]{1,0:T(8,128)(2,1)S(1)}, bf16[32,5248]{1,0:T(8,128)(2,1)S(1)}, u32[]{:S(2)}, u32[]{:S(2)}) collective-permute-start(bf16[32,5248]{1,0:T(8,128)(2,1)S(1)} %get-tuple-element.172), channel_id=1, source_target_pairs={{0,1},{1,0},{2,3},{3,2},{4,5},{5,4},{6,7},{7,6},{8,9},{9,8},{10,11... | collective-permute-start | bytes 1007624 | tf_op jit(solution)/shard_map/ppermute | solution.py:183
  42.2 2.6 %collective-permute-start.13 = (bf16[32,5248]{1,0:T(8,128)(2,1)S(1)}, bf16[32,5248]{1,0:T(8,128)(2,1)S(1)}, u32[]{:S(2)}, u32[]{:S(2)}) collective-permute-start(bf16[32,5248]{1,0:T(8,128)(2,1)S(1)} %get-tuple-element.171), channel_id=1, source_target_pairs={{0,1},{1,0},{2,3},{3,2},{4,5},{5,4},{6,7},{7,6},{8,9},{9,8},{10,11... | collective-permute-start | bytes 1007624 | tf_op jit(solution)/shard_map/ppermute | solution.py:183
  42.7 23.7 %collective-permute-start.8 = (bf16[64,5248]{1,0:T(8,128)(2,1)S(1)}, bf16[64,5248]{1,0:T(8,128)(2,1)S(1)}, u32[]{:S(2)}, u32[]{:S(2)}) collective-permute-start(bf16[64,5248]{1,0:T(8,128)(2,1)S(1)} %collective-permute-done.refs_0_), channel_id=1, source_target_pairs={{0,4},{1,13},{2,6},{3,15},{4,8},{5,1},{6,10},{7,3},{8,12},{9,5},{1... | collective-permute-start | bytes 2015240 | tf_op jit(solution)/shard_map/ppermute | solution.py:183
  44.3 22.1 %collective-permute-start.9 = (bf16[64,5248]{1,0:T(8,128)(2,1)S(1)}, bf16[64,5248]{1,0:T(8,128)(2,1)S(1)}, u32[]{:S(2)}, u32[]{:S(2)}) collective-permute-start(bf16[64,5248]{1,0:T(8,128)(2,1)S(1)} %collective-permute-done.refs_0_), channel_id=1, source_target_pairs={{0,2},{1,3},{2,0},{3,1},{4,6},{5,7},{6,4},{7,5},{8,10},{9,11},{10,... | collective-permute-start | bytes 2015240 | tf_op jit(solution)/shard_map/ppermute | solution.py:183
  44.8 14.4 %slice-start = ((s8[8847360]{0:T(1024)(128)(4,1)}), s8[4194304]{0:T(1024)(128)(4,1)S(1)}, s32[]{:S(2)}) async-start(s8[8847360]{0:T(1024)(128)(4,1)} %bitcast.5), calls=%async_computation.1 | async-start | bytes 8388608
  44.8 3.7 %copy-start.2 = (bf16[864,5120]{1,0:T(8,128)(2,1)S(1)}, bf16[864,5120]{1,0:T(8,128)(2,1)}, u32[]{:S(2)}) copy-start(bf16[864,5120]{1,0:T(8,128)(2,1)} %refs_6_.7) | copy-start | bytes 26542084
  48.5 10.6 %slice-start.1 = ((s8[8847360]{0:T(1024)(128)(4,1)}), s8[4194304]{0:T(1024)(128)(4,1)S(1)}, s32[]{:S(2)}) async-start(s8[8847360]{0:T(1024)(128)(4,1)} %bitcast.5), calls=%async_computation.2 | async-start | bytes 8388608
  48.5 10.6 %slice-start.2 = ((s8[8847360]{0:T(1024)(128)(4,1)}), s8[458752]{0:T(1024)(128)(4,1)S(1)}, s32[]{:S(2)}) async-start(s8[8847360]{0:T(1024)(128)(4,1)} %bitcast.5), calls=%async_computation.3 | async-start | bytes 917504
  48.5 10.6 %slice-start.5 = ((s8[8847360]{0:T(1024)(128)(4,1)}), s8[458752]{0:T(1024)(128)(4,1)S(1)}, s32[]{:S(2)}) async-start(s8[8847360]{0:T(1024)(128)(4,1)} %bitcast.11), calls=%async_computation.6 | async-start | bytes 917504
  53.4 1.8 %collective-permute-start.18 = (bf16[32,5120]{1,0:T(8,128)(2,1)S(1)}, bf16[32,5120]{1,0:T(8,128)(2,1)S(1)}, u32[]{:S(2)}, u32[]{:S(2)}) collective-permute-start(bf16[32,5120]{1,0:T(8,128)(2,1)S(1)} %get-tuple-element.182), channel_id=1, source_target_pairs={{0,1},{1,0},{2,3},{3,2},{4,5},{5,4},{6,7},{7,6},{8,9},{9,8},{10,11... | collective-permute-start | bytes 983048 | tf_op jit(solution)/shard_map/ppermute | solution.py:183
  54.0 1.7 %collective-permute-start.19 = (bf16[32,5120]{1,0:T(8,128)(2,1)S(1)}, bf16[32,5120]{1,0:T(8,128)(2,1)S(1)}, u32[]{:S(2)}, u32[]{:S(2)}) collective-permute-start(bf16[32,5120]{1,0:T(8,128)(2,1)S(1)} %get-tuple-element.181), channel_id=1, source_target_pairs={{0,1},{1,0},{2,3},{3,2},{4,5},{5,4},{6,7},{7,6},{8,9},{9,8},{10,11... | collective-permute-start | bytes 983048 | tf_op jit(solution)/shard_map/ppermute | solution.py:183
  54.1 2.2 %collective-permute-start.14 = (bf16[32,5120]{1,0:T(8,128)(2,1)S(1)}, bf16[32,5120]{1,0:T(8,128)(2,1)S(1)}, u32[]{:S(2)}, u32[]{:S(2)}) collective-permute-start(bf16[32,5120]{1,0:T(8,128)(2,1)S(1)} %get-tuple-element.184), channel_id=1, source_target_pairs={{0,1},{1,0},{2,3},{3,2},{4,5},{5,4},{6,7},{7,6},{8,9},{9,8},{10,11... | collective-permute-start | bytes 983048 | tf_op jit(solution)/shard_map/ppermute | solution.py:183
  55.2 2.5 %collective-permute-start.15 = (bf16[32,5120]{1,0:T(8,128)(2,1)S(1)}, bf16[32,5120]{1,0:T(8,128)(2,1)S(1)}, u32[]{:S(2)}, u32[]{:S(2)}) collective-permute-start(bf16[32,5120]{1,0:T(8,128)(2,1)S(1)} %get-tuple-element.183), channel_id=1, source_target_pairs={{0,1},{1,0},{2,3},{3,2},{4,5},{5,4},{6,7},{7,6},{8,9},{9,8},{10,11... | collective-permute-start | bytes 983048 | tf_op jit(solution)/shard_map/ppermute | solution.py:183
  55.7 22.0 %collective-permute-start.30 = (bf16[64,5120]{1,0:T(8,128)(2,1)S(1)}, bf16[64,5120]{1,0:T(8,128)(2,1)S(1)}, u32[]{:S(2)}, u32[]{:S(2)}) collective-permute-start(bf16[64,5120]{1,0:T(8,128)(2,1)S(1)} %collective-permute-done.16.refs_0_), channel_id=1, source_target_pairs={{0,4},{1,13},{2,6},{3,15},{4,8},{5,1},{6,10},{7,3},{8,12},{9,5},{1... | collective-permute-start | bytes 1966088 | tf_op jit(solution)/shard_map/ppermute | solution.py:183
  56.3 21.4 %collective-permute-start.31 = (bf16[64,5120]{1,0:T(8,128)(2,1)S(1)}, bf16[64,5120]{1,0:T(8,128)(2,1)S(1)}, u32[]{:S(2)}, u32[]{:S(2)}) collective-permute-start(bf16[64,5120]{1,0:T(8,128)(2,1)S(1)} %collective-permute-done.16.refs_0_), channel_id=1, source_target_pairs={{0,2},{1,3},{2,0},{3,1},{4,6},{5,7},{6,4},{7,5},{8,10},{9,11},{10,... | collective-permute-start | bytes 1966088 | tf_op jit(solution)/shard_map/ppermute | solution.py:183
  57.7 12.6 %slice-start.6 = ((s8[8847360]{0:T(1024)(128)(4,1)}), s8[4194304]{0:T(1024)(128)(4,1)S(1)}, s32[]{:S(2)}) async-start(s8[8847360]{0:T(1024)(128)(4,1)} %bitcast.16), calls=%async_computation.7 | async-start | bytes 8388608
  57.7 12.6 %slice-start.7 = ((s8[8847360]{0:T(1024)(128)(4,1)}), s8[4194304]{0:T(1024)(128)(4,1)S(1)}, s32[]{:S(2)}) async-start(s8[8847360]{0:T(1024)(128)(4,1)} %bitcast.16), calls=%async_computation.8 | async-start | bytes 8388608
  57.7 12.6 %slice-start.8 = ((s8[8847360]{0:T(1024)(128)(4,1)}), s8[458752]{0:T(1024)(128)(4,1)S(1)}, s32[]{:S(2)}) async-start(s8[8847360]{0:T(1024)(128)(4,1)} %bitcast.16), calls=%async_computation.9 | async-start | bytes 917504
  57.7 9.4 %collective-permute-start.22 = (bf16[32,5248]{1,0:T(8,128)(2,1)S(1)}, bf16[32,5248]{1,0:T(8,128)(2,1)S(1)}, u32[]{:S(2)}, u32[]{:S(2)}) collective-permute-start(bf16[32,5248]{1,0:T(8,128)(2,1)S(1)} %get-tuple-element.170), channel_id=1, source_target_pairs={{0,1},{1,0},{2,3},{3,2},{4,5},{5,4},{6,7},{7,6},{8,9},{9,8},{10,11... | collective-permute-start | bytes 1007624 | tf_op jit(solution)/shard_map/ppermute | solution.py:183
  66.4 1.7 %collective-permute-start.26 = (bf16[32,5248]{1,0:T(8,128)(2,1)S(1)}, bf16[32,5248]{1,0:T(8,128)(2,1)S(1)}, u32[]{:S(2)}, u32[]{:S(2)}) collective-permute-start(bf16[32,5248]{1,0:T(8,128)(2,1)S(1)} %get-tuple-element.166), channel_id=1, source_target_pairs={{0,1},{1,0},{2,3},{3,2},{4,5},{5,4},{6,7},{7,6},{8,9},{9,8},{10,11... | collective-permute-start | bytes 1007624 | tf_op jit(solution)/shard_map/ppermute | solution.py:183
  66.5 2.1 %collective-permute-start.27 = (bf16[32,5248]{1,0:T(8,128)(2,1)S(1)}, bf16[32,5248]{1,0:T(8,128)(2,1)S(1)}, u32[]{:S(2)}, u32[]{:S(2)}) collective-permute-start(bf16[32,5248]{1,0:T(8,128)(2,1)S(1)} %get-tuple-element.165), channel_id=1, source_target_pairs={{0,1},{1,0},{2,3},{3,2},{4,5},{5,4},{6,7},{7,6},{8,9},{9,8},{10,11... | collective-permute-start | bytes 1007624 | tf_op jit(solution)/shard_map/ppermute | solution.py:183
  67.1 2.0 %collective-permute-start.23 = (bf16[32,5248]{1,0:T(8,128)(2,1)S(1)}, bf16[32,5248]{1,0:T(8,128)(2,1)S(1)}, u32[]{:S(2)}, u32[]{:S(2)}) collective-permute-start(bf16[32,5248]{1,0:T(8,128)(2,1)S(1)} %get-tuple-element.169), channel_id=1, source_target_pairs={{0,1},{1,0},{2,3},{3,2},{4,5},{5,4},{6,7},{7,6},{8,9},{9,8},{10,11... | collective-permute-start | bytes 1007624 | tf_op jit(solution)/shard_map/ppermute | solution.py:183
  68.2 1.6 %collective-permute-start.24 = (bf16[32,5248]{1,0:T(8,128)(2,1)S(1)}, bf16[32,5248]{1,0:T(8,128)(2,1)S(1)}, u32[]{:S(2)}, u32[]{:S(2)}) collective-permute-start(bf16[32,5248]{1,0:T(8,128)(2,1)S(1)} %get-tuple-element.168), channel_id=1, source_target_pairs={{0,1},{1,0},{2,3},{3,2},{4,5},{5,4},{6,7},{7,6},{8,9},{9,8},{10,11... | collective-permute-start | bytes 1007624 | tf_op jit(solution)/shard_map/ppermute | solution.py:183
  68.6 1.6 %collective-permute-start.25 = (bf16[32,5248]{1,0:T(8,128)(2,1)S(1)}, bf16[32,5248]{1,0:T(8,128)(2,1)S(1)}, u32[]{:S(2)}, u32[]{:S(2)}) collective-permute-start(bf16[32,5248]{1,0:T(8,128)(2,1)S(1)} %get-tuple-element.167), channel_id=1, source_target_pairs={{0,1},{1,0},{2,3},{3,2},{4,5},{5,4},{6,7},{7,6},{8,9},{9,8},{10,11... | collective-permute-start | bytes 1007624 | tf_op jit(solution)/shard_map/ppermute | solution.py:183
  69.1 23.0 %collective-permute-start.21 = (bf16[64,5248]{1,0:T(8,128)(2,1)S(1)}, bf16[64,5248]{1,0:T(8,128)(2,1)S(1)}, u32[]{:S(2)}, u32[]{:S(2)}) collective-permute-start(bf16[64,5248]{1,0:T(8,128)(2,1)S(1)} %collective-permute-done.8.refs_0_), channel_id=1, source_target_pairs={{0,4},{1,13},{2,6},{3,15},{4,8},{5,1},{6,10},{7,3},{8,12},{9,5},{1... | collective-permute-start | bytes 2015240 | tf_op jit(solution)/shard_map/ppermute | solution.py:183
  77.7 16.9 %collective-permute-start.39 = (bf16[64,5120]{1,0:T(8,128)(2,1)S(1)}, bf16[64,5120]{1,0:T(8,128)(2,1)S(1)}, u32[]{:S(2)}, u32[]{:S(2)}) collective-permute-start(bf16[64,5120]{1,0:T(8,128)(2,1)S(1)} %collective-permute-done.30.refs_3_), channel_id=1, source_target_pairs={{0,2},{1,3},{2,0},{3,1},{4,6},{5,7},{6,4},{7,5},{8,10},{9,11},{10,... | collective-permute-start | bytes 1966088 | tf_op jit(solution)/shard_map/ppermute | solution.py:183
  79.5 1.6 %collective-permute-start.32 = (bf16[32,5120]{1,0:T(8,128)(2,1)S(1)}, bf16[32,5120]{1,0:T(8,128)(2,1)S(1)}, u32[]{:S(2)}, u32[]{:S(2)}) collective-permute-start(bf16[32,5120]{1,0:T(8,128)(2,1)S(1)} %get-tuple-element.178), channel_id=1, source_target_pairs={{0,1},{1,0},{2,3},{3,2},{4,5},{5,4},{6,7},{7,6},{8,9},{9,8},{10,11... | collective-permute-start | bytes 983048 | tf_op jit(solution)/shard_map/ppermute | solution.py:183
  79.5 2.1 %collective-permute-start.33 = (bf16[32,5120]{1,0:T(8,128)(2,1)S(1)}, bf16[32,5120]{1,0:T(8,128)(2,1)S(1)}, u32[]{:S(2)}, u32[]{:S(2)}) collective-permute-start(bf16[32,5120]{1,0:T(8,128)(2,1)S(1)} %get-tuple-element.177), channel_id=1, source_target_pairs={{0,1},{1,0},{2,3},{3,2},{4,5},{5,4},{6,7},{7,6},{8,9},{9,8},{10,11... | collective-permute-start | bytes 983048 | tf_op jit(solution)/shard_map/ppermute | solution.py:183
  80.1 2.0 %collective-permute-start.34 = (bf16[32,5120]{1,0:T(8,128)(2,1)S(1)}, bf16[32,5120]{1,0:T(8,128)(2,1)S(1)}, u32[]{:S(2)}, u32[]{:S(2)}) collective-permute-start(bf16[32,5120]{1,0:T(8,128)(2,1)S(1)} %get-tuple-element.176), channel_id=1, source_target_pairs={{0,1},{1,0},{2,3},{3,2},{4,5},{5,4},{6,7},{7,6},{8,9},{9,8},{10,11... | collective-permute-start | bytes 983048 | tf_op jit(solution)/shard_map/ppermute | solution.py:183
  81.2 1.6 %collective-permute-start.35 = (bf16[32,5120]{1,0:T(8,128)(2,1)S(1)}, bf16[32,5120]{1,0:T(8,128)(2,1)S(1)}, u32[]{:S(2)}, u32[]{:S(2)}) collective-permute-start(bf16[32,5120]{1,0:T(8,128)(2,1)S(1)} %get-tuple-element.175), channel_id=1, source_target_pairs={{0,1},{1,0},{2,3},{3,2},{4,5},{5,4},{6,7},{7,6},{8,9},{9,8},{10,11... | collective-permute-start | bytes 983048 | tf_op jit(solution)/shard_map/ppermute | solution.py:183
  81.6 1.6 %collective-permute-start.28 = (bf16[32,5120]{1,0:T(8,128)(2,1)S(1)}, bf16[32,5120]{1,0:T(8,128)(2,1)S(1)}, u32[]{:S(2)}, u32[]{:S(2)}) collective-permute-start(bf16[32,5120]{1,0:T(8,128)(2,1)S(1)} %get-tuple-element.180), channel_id=1, source_target_pairs={{0,1},{1,0},{2,3},{3,2},{4,5},{5,4},{6,7},{7,6},{8,9},{9,8},{10,11... | collective-permute-start | bytes 983048 | tf_op jit(solution)/shard_map/ppermute | solution.py:183
  82.1 1.6 %collective-permute-start.29 = (bf16[32,5120]{1,0:T(8,128)(2,1)S(1)}, bf16[32,5120]{1,0:T(8,128)(2,1)S(1)}, u32[]{:S(2)}, u32[]{:S(2)}) collective-permute-start(bf16[32,5120]{1,0:T(8,128)(2,1)S(1)} %get-tuple-element.179), channel_id=1, source_target_pairs={{0,1},{1,0},{2,3},{3,2},{4,5},{5,4},{6,7},{7,6},{8,9},{9,8},{10,11... | collective-permute-start | bytes 983048 | tf_op jit(solution)/shard_map/ppermute | solution.py:183
  82.8 26.0 %collective-permute-start.20 = (bf16[64,5248]{1,0:T(8,128)(2,1)S(1)}, bf16[64,5248]{1,0:T(8,128)(2,1)S(1)}, u32[]{:S(2)}, u32[]{:S(2)}) collective-permute-start(bf16[64,5248]{1,0:T(8,128)(2,1)S(1)} %collective-permute-done.9.refs_3_), channel_id=1, source_target_pairs={{0,4},{1,13},{2,6},{3,15},{4,8},{5,1},{6,10},{7,3},{8,12},{9,5},{1... | collective-permute-start | bytes 2015240 | tf_op jit(solution)/shard_map/ppermute | solution.py:183
  92.1 16.9 %collective-permute-start.36 = (bf16[64,5248]{1,0:T(8,128)(2,1)S(1)}, bf16[64,5248]{1,0:T(8,128)(2,1)S(1)}, u32[]{:S(2)}, u32[]{:S(2)}) collective-permute-start(bf16[64,5248]{1,0:T(8,128)(2,1)S(1)} %collective-permute-done.21.refs_3_), channel_id=1, source_target_pairs={{0,2},{1,3},{2,0},{3,1},{4,6},{5,7},{6,4},{7,5},{8,10},{9,11},{10,... | collective-permute-start | bytes 2015240 | tf_op jit(solution)/shard_map/ppermute | solution.py:183
  94.6 7.6 %collective-permute-start.40 = (bf16[64,5120]{1,0:T(8,128)(2,1)S(1)}, bf16[64,5120]{1,0:T(8,128)(2,1)S(1)}, u32[]{:S(2)}, u32[]{:S(2)}) collective-permute-start(bf16[64,5120]{1,0:T(8,128)(2,1)S(1)} %collective-permute-done.39.refs_3_), channel_id=1, source_target_pairs={{0,1},{1,0},{2,3},{3,2},{4,5},{5,4},{6,7},{7,6},{8,9},{9,8},{10,11... | collective-permute-start | bytes 1966088 | tf_op jit(solution)/shard_map/ppermute | solution.py:183
  94.6 2.5 %collective-permute-start.37 = (bf16[32,5248]{1,0:T(8,128)(2,1)S(1)}, bf16[32,5248]{1,0:T(8,128)(2,1)S(1)}, u32[]{:S(2)}, u32[]{:S(2)}) collective-permute-start(bf16[32,5248]{1,0:T(8,128)(2,1)S(1)} %get-tuple-element.164), channel_id=1, source_target_pairs={{0,1},{1,0},{2,3},{3,2},{4,5},{5,4},{6,7},{7,6},{8,9},{9,8},{10,11... | collective-permute-start | bytes 1007624 | tf_op jit(solution)/shard_map/ppermute | solution.py:183
  95.2 2.4 %collective-permute-start.38 = (bf16[32,5248]{1,0:T(8,128)(2,1)S(1)}, bf16[32,5248]{1,0:T(8,128)(2,1)S(1)}, u32[]{:S(2)}, u32[]{:S(2)}) collective-permute-start(bf16[32,5248]{1,0:T(8,128)(2,1)S(1)} %get-tuple-element.163), channel_id=1, source_target_pairs={{0,1},{1,0},{2,3},{3,2},{4,5},{5,4},{6,7},{7,6},{8,9},{9,8},{10,11... | collective-permute-start | bytes 1007624 | tf_op jit(solution)/shard_map/ppermute | solution.py:183
  109.1 1.7 %collective-permute-start.41 = (bf16[32,5248]{1,0:T(8,128)(2,1)S(1)}, bf16[32,5248]{1,0:T(8,128)(2,1)S(1)}, u32[]{:S(2)}, u32[]{:S(2)}) collective-permute-start(bf16[32,5248]{1,0:T(8,128)(2,1)S(1)} %get-tuple-element.162), channel_id=1, source_target_pairs={{0,1},{1,0},{2,3},{3,2},{4,5},{5,4},{6,7},{7,6},{8,9},{9,8},{10,11... | collective-permute-start | bytes 1007624 | tf_op jit(solution)/shard_map/ppermute | solution.py:183
  109.1 2.1 %collective-permute-start.42 = (bf16[32,5248]{1,0:T(8,128)(2,1)S(1)}, bf16[32,5248]{1,0:T(8,128)(2,1)S(1)}, u32[]{:S(2)}, u32[]{:S(2)}) collective-permute-start(bf16[32,5248]{1,0:T(8,128)(2,1)S(1)} %get-tuple-element.161), channel_id=1, source_target_pairs={{0,1},{1,0},{2,3},{3,2},{4,5},{5,4},{6,7},{7,6},{8,9},{9,8},{10,11... | collective-permute-start | bytes 1007624 | tf_op jit(solution)/shard_map/ppermute | solution.py:183
  109.7 2.0 %collective-permute-start.43 = (bf16[32,5248]{1,0:T(8,128)(2,1)S(1)}, bf16[32,5248]{1,0:T(8,128)(2,1)S(1)}, u32[]{:S(2)}, u32[]{:S(2)}) collective-permute-start(bf16[32,5248]{1,0:T(8,128)(2,1)S(1)} %get-tuple-element.160), channel_id=1, source_target_pairs={{0,1},{1,0},{2,3},{3,2},{4,5},{5,4},{6,7},{7,6},{8,9},{9,8},{10,11... | collective-permute-start | bytes 1007624 | tf_op jit(solution)/shard_map/ppermute | solution.py:183
  109.8 2.4 %collective-permute-start.44 = (bf16[32,5248]{1,0:T(8,128)(2,1)S(1)}, bf16[32,5248]{1,0:T(8,128)(2,1)S(1)}, u32[]{:S(2)}, u32[]{:S(2)}) collective-permute-start(bf16[32,5248]{1,0:T(8,128)(2,1)S(1)} %get-tuple-element.159), channel_id=1, source_target_pairs={{0,1},{1,0},{2,3},{3,2},{4,5},{5,4},{6,7},{7,6},{8,9},{9,8},{10,11... | collective-permute-start | bytes 1007624 | tf_op jit(solution)/shard_map/ppermute | solution.py:183
  117.0 1.4 %collective-permute-start.45 = (bf16[128,512]{1,0:T(8,128)(2,1)S(1)}, bf16[128,512]{1,0:T(8,128)(2,1)S(1)}, u32[]{:S(2)}, u32[]{:S(2)}) collective-permute-start(bf16[128,512]{1,0:T(8,128)(2,1)S(1)} %slice.15), channel_id=1, source_target_pairs={{0,1},{1,0},{2,3},{3,2},{4,5},{5,4},{6,7},{7,6},{8,9},{9,8},{10,11... | collective-permute-start | bytes 393224 | tf_op jit(solution)/shard_map/ppermute | solution.py:183
where the time goes:
time: 131 us
  Pallas kernels  47.4 us (36%)
  waiting for transfers between devices  27.7 us (21%)
  starting transfers between devices  27.3 us (21%)
  local copies, waits for them, and re-layouts  12.3 us (9%)
  blocking collectives  11.6 us (9%)
  other arithmetic  4.13 us (3%)
    pallas_call x8, Pallas kernels, on_chip(): pl.pallas_call(lambda *refs: kernel(len(pieces), *refs), in_specs=[vmem]...  47.4 us
    ppermute x46, waiting for transfers between devices, move(): return lax.ppermute(value, 'fsdp', pairs)  27.7 us
    ppermute x46, starting transfers between devices, move(): return lax.ppermute(value, 'fsdp', pairs)  27.3 us
    all_to_all x1, blocking collectives, on_device(): parts = lax.all_to_all(parts, 'fsdp', 0, 0, axis_index_groups=chips)  11.6 us
    unnamed x30, local copies, waits for them, and re-layouts  10.7 us
  transfers between devices with their start and end apart: 46, of which 29 were waited for; matrix products, arithmetic and copies ran while one was open for 4% of the time, Pallas kernels for 33%

commit v1 on v0

--- a/solution.py
+++ b/solution.py
@@ -246,8 +246,8 @@
         rows_in = [across_in, *swapped_across, corner_in, *swapped_corner]
         saved = first_side(rows_in, width)
         across_out, corner_out, total, saved = after((coming_out[1], coming_last, total, saved))
-        swapped_out = swap(across_out)
-        rows_out = [across_out, *swapped_out, corner_out, *swap(corner_out)]
+        swapped_out = swap(across_out, 1)
+        rows_out = [across_out, *swapped_out, corner_out, *swap(corner_out, 1)]
         total = other_side(rows_out, saved, total, width)
     else:
         gather = lambda piece: lax.all_gather(piece, "fsdp", axis=0, tiled=True)

time: 131 us -> 131 us (level)
    ppermute x46 -> x44, waiting for transfers between devices: 27.7 us -> 28.3 us  [move(): return lax.ppermute(value, 'fsdp', pairs)]
    ppermute x46 -> x44, starting transfers between devices: 27.3 us -> 26.7 us  [move(): return lax.ppermute(value, 'fsdp', pairs)]
  transfers between devices with their start and end apart: 46 -> 44, of which waited for: 29 -> 27; matrix products, arithmetic and copies ran while one was open for 4% -> 4% of each run, Pallas kernels for 33% -> 33%
where the time goes in v1:
time: 131 us
  Pallas kernels  47.4 us (36%)
  waiting for transfers between devices  28.3 us (22%)
  starting transfers between devices  26.7 us (20%)
  local copies, waits for them, and re-layouts  12.2 us (9%)
  blocking collectives  11.6 us (9%)
  other arithmetic  4.13 us (3%)
    pallas_call x8, Pallas kernels, on_chip(): pl.pallas_call(lambda *refs: kernel(len(pieces), *refs), in_specs=[vmem]...  47.4 us
    ppermute x44, waiting for transfers between devices, move(): return lax.ppermute(value, 'fsdp', pairs)  28.3 us
    ppermute x44, starting transfers between devices, move(): return lax.ppermute(value, 'fsdp', pairs)  26.7 us
    all_to_all x1, blocking collectives, on_device(): parts = lax.all_to_all(parts, 'fsdp', 0, 0, axis_index_groups=chips)  11.6 us
    unnamed x30, local copies, waits for them, and re-layouts  10.7 us
  transfers between devices with their start and end apart: 44, of which 27 were waited for; matrix products, arithmetic and copies ran while one was open for 4% of the time, Pallas kernels for 33%

profile of v1, /device:TPU:0, one launch (start us, length us, event | category | flops | bytes accessed | tf_op | source)
XLA Modules:
  0.0 130.7 jit_solution(16782439940927596392)
XLA Ops:
  0.0 3.0 %collective-permute-start.4 = (bf16[64,5120]{1,0:T(8,128)(2,1)}, bf16[64,5120]{1,0:T(8,128)(2,1)S(1)}, u32[]{:S(2)}, u32[]{:S(2)}) collective-permute-start(bf16[64,5120]{1,0:T(8,128)(2,1)} %refs_0_.1), channel_id=1, source_target_pairs={{0,4},{1,13},{2,6},{3,15},{4,8},{5,1},{6,10},{7,3},{8,12},{9,5},{1... | collective-permute-start | bytes 1966088 | tf_op jit(solution)/shard_map/ppermute | solution.py:183
  3.0 1.5 %collective-permute-start.5 = (bf16[64,5120]{1,0:T(8,128)(2,1)}, bf16[64,5120]{1,0:T(8,128)(2,1)S(1)}, u32[]{:S(2)}, u32[]{:S(2)}) collective-permute-start(bf16[64,5120]{1,0:T(8,128)(2,1)} %refs_0_.1), channel_id=1, source_target_pairs={{0,2},{1,3},{2,0},{3,1},{4,6},{5,7},{6,4},{7,5},{8,10},{9,11},{10,... | collective-permute-start | bytes 1966088 | tf_op jit(solution)/shard_map/ppermute | solution.py:183
  4.5 0.7 convert_element_type.20
  5.2 0.7 add_convert_fusion
  6.0 0.7 add_convert_fusion.1
  6.7 1.4 %fusion.refs_8_.refs_7_.refs_5_ = bf16[256,5120]{1,0:T(8,128)(2,1)S(1)} fusion(s32[5120]{0:T(1024)} %param.18, bf16[5120]{0:T(1024)(128)(2,1)S(1)} %add_convert_fusion), kind=kLoop, calls=%fused_computation.1 | loop fusion | flops 2621440 | bytes 2652160 | tf_op jit(solution)/shard_map/jit(_where)/select_n | solution.py:26
  8.2 0.4 compare_select_fusion.refs_9_.refs_8_.refs_6_
  8.8 1.6 %collective-permute-start = (bf16[64,5248]{1,0:T(8,128)(2,1)S(1)}, bf16[64,5248]{1,0:T(8,128)(2,1)S(1)}, u32[]{:S(2)}, u32[]{:S(2)}) collective-permute-start(bf16[64,5248]{1,0:T(8,128)(2,1)S(1)} %pad_maximum_fusion.refs_0_), channel_id=1, source_target_pairs={{0,4},{1,13},{2,6},{3,15},{4,8},{5,1},{6,10},{7,3},{8,12},{9,5},{1... | collective-permute-start | bytes 2015240 | tf_op jit(solution)/shard_map/ppermute | solution.py:183
  10.4 0.5 collective-permute-start.1
  11.0 9.8 %collective-permute-done.4.refs_0_ = bf16[64,5120]{1,0:T(8,128)(2,1)S(1)} collective-permute-done((bf16[64,5120]{1,0:T(8,128)(2,1)}, bf16[64,5120]{1,0:T(8,128)(2,1)S(1)}, u32[]{:S(2)}, u32[]{:S(2)}) %collective-permute-start.4) | collective-permute-done | bytes 655392 | tf_op jit(solution)/shard_map/ppermute | solution.py:183
  20.9 0.8 collective-permute-start.6
  21.8 0.5 collective-permute-start.2
  22.3 0.6 collective-permute-done.6.refs_4_
  22.9 0.4 collective-permute-start.3
  23.4 1.3 %collective-permute-start.16 = (bf16[64,5120]{1,0:T(8,128)(2,1)S(1)}, bf16[64,5120]{1,0:T(8,128)(2,1)S(1)}, u32[]{:S(2)}, u32[]{:S(2)}) collective-permute-start(bf16[64,5120]{1,0:T(8,128)(2,1)S(1)} %collective-permute-done.4.refs_0_), channel_id=1, source_target_pairs={{0,4},{1,13},{2,6},{3,15},{4,8},{5,1},{6,10},{7,3},{8,12},{9,5},{1... | collective-permute-start | bytes 1966088 | tf_op jit(solution)/shard_map/ppermute | solution.py:183
  24.7 1.5 %collective-permute-start.17 = (bf16[64,5120]{1,0:T(8,128)(2,1)S(1)}, bf16[64,5120]{1,0:T(8,128)(2,1)S(1)}, u32[]{:S(2)}, u32[]{:S(2)}) collective-permute-start(bf16[64,5120]{1,0:T(8,128)(2,1)S(1)} %collective-permute-done.4.refs_0_), channel_id=1, source_target_pairs={{0,2},{1,3},{2,0},{3,1},{4,6},{5,7},{6,4},{7,5},{8,10},{9,11},{10,... | collective-permute-start | bytes 1966088 | tf_op jit(solution)/shard_map/ppermute | solution.py:183
  26.2 3.5 %copy-done = bf16[5120,864]{0,1:T(8,128)(2,1)S(1)} copy-done((bf16[5120,864]{0,1:T(8,128)(2,1)S(1)}, bf16[5120,864]{0,1:T(8,128)(2,1)}, u32[]{:S(2)}) %copy-start) | copy-done | bytes 8847384
  29.7 3.5 %copy-done.1 = bf16[5120,864]{0,1:T(8,128)(2,1)S(1)} copy-done((bf16[5120,864]{0,1:T(8,128)(2,1)S(1)}, bf16[5120,864]{0,1:T(8,128)(2,1)}, u32[]{:S(2)}) %copy-start.1) | copy-done | bytes 8847384
  33.2 7.2 %forward.4 = (f32[256,864]{1,0:T(8,128)S(1)}, f32[256,864]{1,0:T(8,128)S(1)}, bf16[256,256]{1,0:T(8,128)(2,1)S(1)}, bf16[256,256]{1,0:T(8,128)(2,1)S(1)}) custom-call(bf16[64,5120]{1,0:T(8,128)(2,1)S(1)} %copy-done.3, bf16[32,5120]{1,0:T(8,128)(2,1)S(1)} %collective-permute-done.2.refs_1_, bf16[32,5120]{1,0:T(8,128)(2,1)S(1)} %collective-permute-done.3.refs_2_, ...), custom_call_target="tpu_custom_call" | custom-call | tf_op jit(solution)/shard_map/forward/pallas_call | solution.py:135
  40.5 0.4 collective-permute-start.10
  41.1 0.4 collective-permute-start.12
  41.5 0.7 collective-permute-done.10.refs_1_
  42.7 1.6 %collective-permute-start.8 = (bf16[64,5248]{1,0:T(8,128)(2,1)S(1)}, bf16[64,5248]{1,0:T(8,128)(2,1)S(1)}, u32[]{:S(2)}, u32[]{:S(2)}) collective-permute-start(bf16[64,5248]{1,0:T(8,128)(2,1)S(1)} %collective-permute-done.refs_0_), channel_id=1, source_target_pairs={{0,4},{1,13},{2,6},{3,15},{4,8},{5,1},{6,10},{7,3},{8,12},{9,5},{1... | collective-permute-start | bytes 2015240 | tf_op jit(solution)/shard_map/ppermute | solution.py:183
  44.3 0.5 collective-permute-start.9
  44.9 3.7 %copy-done.2 = bf16[864,5120]{1,0:T(8,128)(2,1)S(1)} copy-done((bf16[864,5120]{1,0:T(8,128)(2,1)S(1)}, bf16[864,5120]{1,0:T(8,128)(2,1)}, u32[]{:S(2)}) %copy-start.2) | copy-done | bytes 8847384
  48.5 4.8 %backward.4.refs_13_ = f32[256,512]{1,0:T(8,128)S(1)} custom-call(bf16[64,5248]{1,0:T(8,128)(2,1)S(1)} %pad_maximum_fusion.refs_0_, bf16[32,5248]{1,0:T(8,128)(2,1)S(1)} %collective-permute-done.10.refs_1_, bf16[32,5248]{1,0:T(8,128)(2,1)S(1)} %collective-permute-done.11.refs_2_, bf16[64,5248]{1,0:T(8,128)(2,1)S(1)} %collective-permute-done.1.refs_3_, ...), custom_call_target="tpu_custom_call" | custom-call | tf_op jit(solution)/shard_map/backward/pallas_call | solution.py:135
  53.4 0.6 collective-permute-start.18
  54.1 0.5 collective-permute-start.14
  54.6 0.6 collective-permute-done.18.refs_4_
  55.2 0.4 collective-permute-start.15
  55.7 0.5 collective-permute-start.30
  56.3 1.4 %collective-permute-start.31 = (bf16[64,5120]{1,0:T(8,128)(2,1)S(1)}, bf16[64,5120]{1,0:T(8,128)(2,1)S(1)}, u32[]{:S(2)}, u32[]{:S(2)}) collective-permute-start(bf16[64,5120]{1,0:T(8,128)(2,1)S(1)} %collective-permute-done.16.refs_0_), channel_id=1, source_target_pairs={{0,2},{1,3},{2,0},{3,1},{4,6},{5,7},{6,4},{7,5},{8,10},{9,11},{10,... | collective-permute-start | bytes 1966088 | tf_op jit(solution)/shard_map/ppermute | solution.py:183
  57.7 1.4 %collective-permute-start.22 = (bf16[32,5248]{1,0:T(8,128)(2,1)S(1)}, bf16[32,5248]{1,0:T(8,128)(2,1)S(1)}, u32[]{:S(2)}, u32[]{:S(2)}) collective-permute-start(bf16[32,5248]{1,0:T(8,128)(2,1)S(1)} %get-tuple-element.166), channel_id=1, source_target_pairs={{0,1},{1,0},{2,3},{3,2},{4,5},{5,4},{6,7},{7,6},{8,9},{9,8},{10,11... | collective-permute-start | bytes 1007624 | tf_op jit(solution)/shard_map/ppermute | solution.py:183
  59.2 7.2 %forward.5 = (f32[256,864]{1,0:T(8,128)S(1)}, f32[256,864]{1,0:T(8,128)S(1)}, bf16[256,256]{1,0:T(8,128)(2,1)S(1)}, bf16[256,256]{1,0:T(8,128)(2,1)S(1)}) custom-call(bf16[64,5120]{1,0:T(8,128)(2,1)S(1)} %collective-permute-done.4.refs_0_, bf16[32,5120]{1,0:T(8,128)(2,1)S(1)} %collective-permute-done.14.refs_1_, ...), custom_call_target="tpu_custom_call" | custom-call | tf_op jit(solution)/shard_map/forward/pallas_call | solution.py:135
  66.6 0.5 collective-permute-start.27
  67.2 0.9 collective-permute-done.26.refs_1_
  68.3 0.3 collective-permute-done.27.refs_2_
  68.8 0.3 collective-permute-done.23.refs_2_
  69.5 0.3 collective-permute-done.24.refs_4_
  69.8 0.5 collective-permute-done.25.refs_5_
  70.3 4.9 %backward.5.refs_13_ = f32[256,512]{1,0:T(8,128)S(1)} custom-call(bf16[64,5248]{1,0:T(8,128)(2,1)S(1)} %collective-permute-done.refs_0_, bf16[32,5248]{1,0:T(8,128)(2,1)S(1)} %collective-permute-done.22.refs_1_, bf16[32,5248]{1,0:T(8,128)(2,1)S(1)} %collective-permute-done.23.refs_2_, bf16[64,5248]{1,0:T(8,128)(2,1)S(1)} %collective-permute-done.9.refs_3_, ...), custom_call_target="tpu_custom_call" | custom-call | tf_op jit(solution)/shard_map/backward/pallas_call | solution.py:135
  75.2 2.5 %collective-permute-done.30.refs_3_ = bf16[64,5120]{1,0:T(8,128)(2,1)S(1)} collective-permute-done((bf16[64,5120]{1,0:T(8,128)(2,1)S(1)}, bf16[64,5120]{1,0:T(8,128)(2,1)S(1)}, u32[]{:S(2)}, u32[]{:S(2)}) %collective-permute-start.30) | collective-permute-done | bytes 655392 | tf_op jit(solution)/shard_map/ppermute | solution.py:183
  77.7 1.8 %collective-permute-start.39 = (bf16[64,5120]{1,0:T(8,128)(2,1)S(1)}, bf16[64,5120]{1,0:T(8,128)(2,1)S(1)}, u32[]{:S(2)}, u32[]{:S(2)}) collective-permute-start(bf16[64,5120]{1,0:T(8,128)(2,1)S(1)} %collective-permute-done.30.refs_3_), channel_id=1, source_target_pairs={{0,2},{1,3},{2,0},{3,1},{4,6},{5,7},{6,4},{7,5},{8,10},{9,11},{10,... | collective-permute-start | bytes 1966088 | tf_op jit(solution)/shard_map/ppermute | solution.py:183
  79.5 0.5 collective-permute-start.33
  80.2 0.9 collective-permute-done.32.refs_4_
  82.2 0.6 collective-permute-done.35.refs_2_
  82.8 0.5 collective-permute-done.28.refs_1_
  83.3 0.5 collective-permute-done.29.refs_2_
  83.7 7.4 %forward.6 = (f32[256,864]{1,0:T(8,128)S(1)}, f32[256,864]{1,0:T(8,128)S(1)}, bf16[256,256]{1,0:T(8,128)(2,1)S(1)}, bf16[256,256]{1,0:T(8,128)(2,1)S(1)}) custom-call(bf16[64,5120]{1,0:T(8,128)(2,1)S(1)} %collective-permute-done.16.refs_0_, bf16[32,5120]{1,0:T(8,128)(2,1)S(1)} %collective-permute-done.28.refs_1_, ...), custom_call_target="tpu_custom_call" | custom-call | tf_op jit(solution)/shard_map/forward/pallas_call | solution.py:135
  91.1 1.0 collective-permute-done.21.refs_3_
  92.1 1.7 %collective-permute-start.36 = (bf16[64,5248]{1,0:T(8,128)(2,1)S(1)}, bf16[64,5248]{1,0:T(8,128)(2,1)S(1)}, u32[]{:S(2)}, u32[]{:S(2)}) collective-permute-start(bf16[64,5248]{1,0:T(8,128)(2,1)S(1)} %collective-permute-done.21.refs_3_), channel_id=1, source_target_pairs={{0,2},{1,3},{2,0},{3,1},{4,6},{5,7},{6,4},{7,5},{8,10},{9,11},{10,... | collective-permute-start | bytes 2015240 | tf_op jit(solution)/shard_map/ppermute | solution.py:183
  93.8 0.8 collective-permute-done.39.refs_3_
  94.6 0.6 collective-permute-start.37
  95.3 1.9 %collective-permute-done.37.refs_4_ = bf16[32,5248]{1,0:T(8,128)(2,1)S(1)} collective-permute-done((bf16[32,5248]{1,0:T(8,128)(2,1)S(1)}, bf16[32,5248]{1,0:T(8,128)(2,1)S(1)}, u32[]{:S(2)}, u32[]{:S(2)}) %collective-permute-start.37) | collective-permute-done | bytes 335904 | tf_op jit(solution)/shard_map/ppermute | solution.py:183
  97.2 0.5 collective-permute-done.38.refs_5_
  97.7 4.5 %backward.6.refs_11_ = f32[256,512]{1,0:T(8,128)S(1)} custom-call(bf16[64,5248]{1,0:T(8,128)(2,1)S(1)} %collective-permute-done.8.refs_0_, bf16[32,5248]{1,0:T(8,128)(2,1)S(1)} %collective-permute-done.26.refs_1_, bf16[32,5248]{1,0:T(8,128)(2,1)S(1)} %collective-permute-done.27.refs_2_, bf16[64,5248]{1,0:T(8,128)(2,1)S(1)} %collective-permute-done.21.refs_3_, ...), custom_call_target="tpu_custom_call" | custom-call | tf_op jit(solution)/shard_map/backward/pallas_call | solution.py:135
  102.2 6.6 %forward.7 = (f32[256,864]{1,0:T(8,128)S(1)}, f32[256,864]{1,0:T(8,128)S(1)}, bf16[256,256]{1,0:T(8,128)(2,1)S(1)}, bf16[256,256]{1,0:T(8,128)(2,1)S(1)}) custom-call(bf16[64,5120]{1,0:T(8,128)(2,1)S(1)} %collective-permute-done.31.refs_0_, bf16[32,5120]{1,0:T(8,128)(2,1)S(1)} %collective-permute-done.34.refs_1_, ...), custom_call_target="tpu_custom_call" | custom-call | tf_op jit(solution)/shard_map/forward/pallas_call | solution.py:135
  109.1 0.5 collective-permute-start.42
  109.5 1.6 %collective-permute-done.41.refs_1_ = bf16[64,5248]{1,0:T(8,128)(2,1)S(1)} collective-permute-done((bf16[64,5248]{1,0:T(8,128)(2,1)S(1)}, bf16[64,5248]{1,0:T(8,128)(2,1)S(1)}, u32[]{:S(2)}, u32[]{:S(2)}) %collective-permute-start.41) | collective-permute-done | bytes 671776 | tf_op jit(solution)/shard_map/ppermute | solution.py:183
  111.1 1.0 collective-permute-done.42.refs_3_
  112.1 4.8 %backward.7 = f32[256,512]{1,0:T(8,128)S(1)} custom-call(bf16[64,5248]{1,0:T(8,128)(2,1)S(1)} %collective-permute-done.20.refs_0_, bf16[64,5248]{1,0:T(8,128)(2,1)S(1)} %collective-permute-done.41.refs_1_, bf16[64,5248]{1,0:T(8,128)(2,1)S(1)} %collective-permute-done.36.refs_2_, bf16[64,5248]{1,0:T(8,128)(2,1)S(1)} %collective-permute-done.42.refs_3_, ...), custom_call_target="tpu_custom_call" | custom-call | tf_op jit(solution)/shard_map/backward/pallas_call | solution.py:135
  117.1 1.2 collective-permute-done.43
  118.4 11.6 %all_to_all.5 = bf16[8,16,512]{2,1,0:T(8,128)(2,1)S(1)} all-to-all(bf16[8,16,512]{2,1,0:T(8,128)(2,1)S(1)} %bitcast.18), channel_id=1, replica_groups={{0,2,4,6,8,10,12,14},{1,3,5,7,9,11,13,15},{16,18,20,22,24,26,28,30},{17..., dimensions={0} | all-to-all | bytes 262144 | tf_op jit(solution)/shard_map/all_to_all | solution.py:261
  130.1 0.6 copy.11
  (96 shorter events, 4.6 us)
Async XLA Ops:
  0.0 8.2 %copy-start.5 = (s32[3,864]{1,0:T(4,128)S(1)}, s32[3,864]{1,0:T(4,128)}, u32[]{:S(2)}) copy-start(s32[3,864]{1,0:T(4,128)} %param.16) | copy-start | bytes 31108
  0.0 8.7 %copy-start.4 = (bf16[64,5120]{1,0:T(8,128)(2,1)S(1)}, bf16[64,5120]{1,0:T(8,128)(2,1)}, u32[]{:S(2)}) copy-start(bf16[64,5120]{1,0:T(8,128)(2,1)} %param.11) | copy-start | bytes 1966084
  0.0 20.8 %collective-permute-start.4 = (bf16[64,5120]{1,0:T(8,128)(2,1)}, bf16[64,5120]{1,0:T(8,128)(2,1)S(1)}, u32[]{:S(2)}, u32[]{:S(2)}) collective-permute-start(bf16[64,5120]{1,0:T(8,128)(2,1)} %refs_0_.1), channel_id=1, source_target_pairs={{0,4},{1,13},{2,6},{3,15},{4,8},{5,1},{6,10},{7,3},{8,12},{9,5},{1... | collective-permute-start | bytes 1966088 | tf_op jit(solution)/shard_map/ppermute | solution.py:183
  3.0 17.8 %collective-permute-start.5 = (bf16[64,5120]{1,0:T(8,128)(2,1)}, bf16[64,5120]{1,0:T(8,128)(2,1)S(1)}, u32[]{:S(2)}, u32[]{:S(2)}) collective-permute-start(bf16[64,5120]{1,0:T(8,128)(2,1)} %refs_0_.1), channel_id=1, source_target_pairs={{0,2},{1,3},{2,0},{3,1},{4,6},{5,7},{6,4},{7,5},{8,10},{9,11},{10,... | collective-permute-start | bytes 1966088 | tf_op jit(solution)/shard_map/ppermute | solution.py:183
  8.2 13.5 %copy-start.3 = (bf16[64,5120]{1,0:T(8,128)(2,1)S(1)}, bf16[64,5120]{1,0:T(8,128)(2,1)}, u32[]{:S(2)}) copy-start(bf16[64,5120]{1,0:T(8,128)(2,1)} %refs_0_.1) | copy-start | bytes 1966084
  8.8 31.6 %collective-permute-start = (bf16[64,5248]{1,0:T(8,128)(2,1)S(1)}, bf16[64,5248]{1,0:T(8,128)(2,1)S(1)}, u32[]{:S(2)}, u32[]{:S(2)}) collective-permute-start(bf16[64,5248]{1,0:T(8,128)(2,1)S(1)} %pad_maximum_fusion.refs_0_), channel_id=1, source_target_pairs={{0,4},{1,13},{2,6},{3,15},{4,8},{5,1},{6,10},{7,3},{8,12},{9,5},{1... | collective-permute-start | bytes 2015240 | tf_op jit(solution)/shard_map/ppermute | solution.py:183
  10.4 30.0 %collective-permute-start.1 = (bf16[64,5248]{1,0:T(8,128)(2,1)S(1)}, bf16[64,5248]{1,0:T(8,128)(2,1)S(1)}, u32[]{:S(2)}, u32[]{:S(2)}) collective-permute-start(bf16[64,5248]{1,0:T(8,128)(2,1)S(1)} %pad_maximum_fusion.refs_0_), channel_id=1, source_target_pairs={{0,2},{1,3},{2,0},{3,1},{4,6},{5,7},{6,4},{7,5},{8,10},{9,11},{10,... | collective-permute-start | bytes 2015240 | tf_op jit(solution)/shard_map/ppermute | solution.py:183
  20.9 2.0 %collective-permute-start.6 = (bf16[32,5120]{1,0:T(8,128)(2,1)S(1)}, bf16[32,5120]{1,0:T(8,128)(2,1)S(1)}, u32[]{:S(2)}, u32[]{:S(2)}) collective-permute-start(bf16[32,5120]{1,0:T(8,128)(2,1)S(1)} %get-tuple-element.182), channel_id=1, source_target_pairs={{0,1},{1,0},{2,3},{3,2},{4,5},{5,4},{6,7},{7,6},{8,9},{9,8},{10,11... | collective-permute-start | bytes 983048 | tf_op jit(solution)/shard_map/ppermute | solution.py:183
  21.6 1.7 %collective-permute-start.7 = (bf16[32,5120]{1,0:T(8,128)(2,1)S(1)}, bf16[32,5120]{1,0:T(8,128)(2,1)S(1)}, u32[]{:S(2)}, u32[]{:S(2)}) collective-permute-start(bf16[32,5120]{1,0:T(8,128)(2,1)S(1)} %get-tuple-element.181), channel_id=1, source_target_pairs={{0,1},{1,0},{2,3},{3,2},{4,5},{5,4},{6,7},{7,6},{8,9},{9,8},{10,11... | collective-permute-start | bytes 983048 | tf_op jit(solution)/shard_map/ppermute | solution.py:183
  21.8 2.9 %collective-permute-start.2 = (bf16[32,5120]{1,0:T(8,128)(2,1)S(1)}, bf16[32,5120]{1,0:T(8,128)(2,1)S(1)}, u32[]{:S(2)}, u32[]{:S(2)}) collective-permute-start(bf16[32,5120]{1,0:T(8,128)(2,1)S(1)} %get-tuple-element.184), channel_id=1, source_target_pairs={{0,1},{1,0},{2,3},{3,2},{4,5},{5,4},{6,7},{7,6},{8,9},{9,8},{10,11... | collective-permute-start | bytes 983048 | tf_op jit(solution)/shard_map/ppermute | solution.py:183
  22.9 3.3 %collective-permute-start.3 = (bf16[32,5120]{1,0:T(8,128)(2,1)S(1)}, bf16[32,5120]{1,0:T(8,128)(2,1)S(1)}, u32[]{:S(2)}, u32[]{:S(2)}) collective-permute-start(bf16[32,5120]{1,0:T(8,128)(2,1)S(1)} %get-tuple-element.183), channel_id=1, source_target_pairs={{0,1},{1,0},{2,3},{3,2},{4,5},{5,4},{6,7},{7,6},{8,9},{9,8},{10,11... | collective-permute-start | bytes 983048 | tf_op jit(solution)/shard_map/ppermute | solution.py:183
  23.4 30.0 %collective-permute-start.16 = (bf16[64,5120]{1,0:T(8,128)(2,1)S(1)}, bf16[64,5120]{1,0:T(8,128)(2,1)S(1)}, u32[]{:S(2)}, u32[]{:S(2)}) collective-permute-start(bf16[64,5120]{1,0:T(8,128)(2,1)S(1)} %collective-permute-done.4.refs_0_), channel_id=1, source_target_pairs={{0,4},{1,13},{2,6},{3,15},{4,8},{5,1},{6,10},{7,3},{8,12},{9,5},{1... | collective-permute-start | bytes 1966088 | tf_op jit(solution)/shard_map/ppermute | solution.py:183
  24.7 28.7 %collective-permute-start.17 = (bf16[64,5120]{1,0:T(8,128)(2,1)S(1)}, bf16[64,5120]{1,0:T(8,128)(2,1)S(1)}, u32[]{:S(2)}, u32[]{:S(2)}) collective-permute-start(bf16[64,5120]{1,0:T(8,128)(2,1)S(1)} %collective-permute-done.4.refs_0_), channel_id=1, source_target_pairs={{0,2},{1,3},{2,0},{3,1},{4,6},{5,7},{6,4},{7,5},{8,10},{9,11},{10,... | collective-permute-start | bytes 1966088 | tf_op jit(solution)/shard_map/ppermute | solution.py:183
  26.2 3.5 %copy-start = (bf16[5120,864]{0,1:T(8,128)(2,1)S(1)}, bf16[5120,864]{0,1:T(8,128)(2,1)}, u32[]{:S(2)}) copy-start(bf16[5120,864]{0,1:T(8,128)(2,1)} %param.13) | copy-start | bytes 26542084
  29.7 3.5 %copy-start.1 = (bf16[5120,864]{0,1:T(8,128)(2,1)S(1)}, bf16[5120,864]{0,1:T(8,128)(2,1)}, u32[]{:S(2)}) copy-start(bf16[5120,864]{0,1:T(8,128)(2,1)} %param.14) | copy-start | bytes 26542084
  33.2 25.9 %slice-start.3 = ((s8[8847360]{0:T(1024)(128)(4,1)}), s8[4194304]{0:T(1024)(128)(4,1)S(1)}, s32[]{:S(2)}) async-start(s8[8847360]{0:T(1024)(128)(4,1)} %bitcast.11), calls=%async_computation.4 | async-start | bytes 8388608
  33.2 25.9 %slice-start.4 = ((s8[8847360]{0:T(1024)(128)(4,1)}), s8[4194304]{0:T(1024)(128)(4,1)S(1)}, s32[]{:S(2)}) async-start(s8[8847360]{0:T(1024)(128)(4,1)} %bitcast.11), calls=%async_computation.5 | async-start | bytes 8388608
  40.5 1.7 %collective-permute-start.10 = (bf16[32,5248]{1,0:T(8,128)(2,1)S(1)}, bf16[32,5248]{1,0:T(8,128)(2,1)S(1)}, u32[]{:S(2)}, u32[]{:S(2)}) collective-permute-start(bf16[32,5248]{1,0:T(8,128)(2,1)S(1)} %get-tuple-element.170), channel_id=1, source_target_pairs={{0,1},{1,0},{2,3},{3,2},{4,5},{5,4},{6,7},{7,6},{8,9},{9,8},{10,11... | collective-permute-start | bytes 1007624 | tf_op jit(solution)/shard_map/ppermute | solution.py:183
  40.9 1.8 %collective-permute-start.11 = (bf16[32,5248]{1,0:T(8,128)(2,1)S(1)}, bf16[32,5248]{1,0:T(8,128)(2,1)S(1)}, u32[]{:S(2)}, u32[]{:S(2)}) collective-permute-start(bf16[32,5248]{1,0:T(8,128)(2,1)S(1)} %get-tuple-element.169), channel_id=1, source_target_pairs={{0,1},{1,0},{2,3},{3,2},{4,5},{5,4},{6,7},{7,6},{8,9},{9,8},{10,11... | collective-permute-start | bytes 1007624 | tf_op jit(solution)/shard_map/ppermute | solution.py:183
  41.1 3.1 %collective-permute-start.12 = (bf16[32,5248]{1,0:T(8,128)(2,1)S(1)}, bf16[32,5248]{1,0:T(8,128)(2,1)S(1)}, u32[]{:S(2)}, u32[]{:S(2)}) collective-permute-start(bf16[32,5248]{1,0:T(8,128)(2,1)S(1)} %get-tuple-element.168), channel_id=1, source_target_pairs={{0,1},{1,0},{2,3},{3,2},{4,5},{5,4},{6,7},{7,6},{8,9},{9,8},{10,11... | collective-permute-start | bytes 1007624 | tf_op jit(solution)/shard_map/ppermute | solution.py:183
  42.2 2.6 %collective-permute-start.13 = (bf16[32,5248]{1,0:T(8,128)(2,1)S(1)}, bf16[32,5248]{1,0:T(8,128)(2,1)S(1)}, u32[]{:S(2)}, u32[]{:S(2)}) collective-permute-start(bf16[32,5248]{1,0:T(8,128)(2,1)S(1)} %get-tuple-element.167), channel_id=1, source_target_pairs={{0,1},{1,0},{2,3},{3,2},{4,5},{5,4},{6,7},{7,6},{8,9},{9,8},{10,11... | collective-permute-start | bytes 1007624 | tf_op jit(solution)/shard_map/ppermute | solution.py:183
  42.7 23.7 %collective-permute-start.8 = (bf16[64,5248]{1,0:T(8,128)(2,1)S(1)}, bf16[64,5248]{1,0:T(8,128)(2,1)S(1)}, u32[]{:S(2)}, u32[]{:S(2)}) collective-permute-start(bf16[64,5248]{1,0:T(8,128)(2,1)S(1)} %collective-permute-done.refs_0_), channel_id=1, source_target_pairs={{0,4},{1,13},{2,6},{3,15},{4,8},{5,1},{6,10},{7,3},{8,12},{9,5},{1... | collective-permute-start | bytes 2015240 | tf_op jit(solution)/shard_map/ppermute | solution.py:183
  44.3 22.1 %collective-permute-start.9 = (bf16[64,5248]{1,0:T(8,128)(2,1)S(1)}, bf16[64,5248]{1,0:T(8,128)(2,1)S(1)}, u32[]{:S(2)}, u32[]{:S(2)}) collective-permute-start(bf16[64,5248]{1,0:T(8,128)(2,1)S(1)} %collective-permute-done.refs_0_), channel_id=1, source_target_pairs={{0,2},{1,3},{2,0},{3,1},{4,6},{5,7},{6,4},{7,5},{8,10},{9,11},{10,... | collective-permute-start | bytes 2015240 | tf_op jit(solution)/shard_map/ppermute | solution.py:183
  44.8 14.4 %slice-start = ((s8[8847360]{0:T(1024)(128)(4,1)}), s8[4194304]{0:T(1024)(128)(4,1)S(1)}, s32[]{:S(2)}) async-start(s8[8847360]{0:T(1024)(128)(4,1)} %bitcast.5), calls=%async_computation.1 | async-start | bytes 8388608
  44.8 3.7 %copy-start.2 = (bf16[864,5120]{1,0:T(8,128)(2,1)S(1)}, bf16[864,5120]{1,0:T(8,128)(2,1)}, u32[]{:S(2)}) copy-start(bf16[864,5120]{1,0:T(8,128)(2,1)} %refs_4_.1) | copy-start | bytes 26542084
  48.5 10.6 %slice-start.1 = ((s8[8847360]{0:T(1024)(128)(4,1)}), s8[4194304]{0:T(1024)(128)(4,1)S(1)}, s32[]{:S(2)}) async-start(s8[8847360]{0:T(1024)(128)(4,1)} %bitcast.5), calls=%async_computation.2 | async-start | bytes 8388608
  48.5 10.6 %slice-start.2 = ((s8[8847360]{0:T(1024)(128)(4,1)}), s8[458752]{0:T(1024)(128)(4,1)S(1)}, s32[]{:S(2)}) async-start(s8[8847360]{0:T(1024)(128)(4,1)} %bitcast.5), calls=%async_computation.3 | async-start | bytes 917504
  48.5 10.6 %slice-start.5 = ((s8[8847360]{0:T(1024)(128)(4,1)}), s8[458752]{0:T(1024)(128)(4,1)S(1)}, s32[]{:S(2)}) async-start(s8[8847360]{0:T(1024)(128)(4,1)} %bitcast.11), calls=%async_computation.6 | async-start | bytes 917504
  53.4 1.8 %collective-permute-start.18 = (bf16[32,5120]{1,0:T(8,128)(2,1)S(1)}, bf16[32,5120]{1,0:T(8,128)(2,1)S(1)}, u32[]{:S(2)}, u32[]{:S(2)}) collective-permute-start(bf16[32,5120]{1,0:T(8,128)(2,1)S(1)} %get-tuple-element.178), channel_id=1, source_target_pairs={{0,1},{1,0},{2,3},{3,2},{4,5},{5,4},{6,7},{7,6},{8,9},{9,8},{10,11... | collective-permute-start | bytes 983048 | tf_op jit(solution)/shard_map/ppermute | solution.py:183
  54.0 1.7 %collective-permute-start.19 = (bf16[32,5120]{1,0:T(8,128)(2,1)S(1)}, bf16[32,5120]{1,0:T(8,128)(2,1)S(1)}, u32[]{:S(2)}, u32[]{:S(2)}) collective-permute-start(bf16[32,5120]{1,0:T(8,128)(2,1)S(1)} %get-tuple-element.177), channel_id=1, source_target_pairs={{0,1},{1,0},{2,3},{3,2},{4,5},{5,4},{6,7},{7,6},{8,9},{9,8},{10,11... | collective-permute-start | bytes 983048 | tf_op jit(solution)/shard_map/ppermute | solution.py:183
  54.1 2.2 %collective-permute-start.14 = (bf16[32,5120]{1,0:T(8,128)(2,1)S(1)}, bf16[32,5120]{1,0:T(8,128)(2,1)S(1)}, u32[]{:S(2)}, u32[]{:S(2)}) collective-permute-start(bf16[32,5120]{1,0:T(8,128)(2,1)S(1)} %get-tuple-element.180), channel_id=1, source_target_pairs={{0,1},{1,0},{2,3},{3,2},{4,5},{5,4},{6,7},{7,6},{8,9},{9,8},{10,11... | collective-permute-start | bytes 983048 | tf_op jit(solution)/shard_map/ppermute | solution.py:183
  55.2 2.5 %collective-permute-start.15 = (bf16[32,5120]{1,0:T(8,128)(2,1)S(1)}, bf16[32,5120]{1,0:T(8,128)(2,1)S(1)}, u32[]{:S(2)}, u32[]{:S(2)}) collective-permute-start(bf16[32,5120]{1,0:T(8,128)(2,1)S(1)} %get-tuple-element.179), channel_id=1, source_target_pairs={{0,1},{1,0},{2,3},{3,2},{4,5},{5,4},{6,7},{7,6},{8,9},{9,8},{10,11... | collective-permute-start | bytes 983048 | tf_op jit(solution)/shard_map/ppermute | solution.py:183
  55.7 22.0 %collective-permute-start.30 = (bf16[64,5120]{1,0:T(8,128)(2,1)S(1)}, bf16[64,5120]{1,0:T(8,128)(2,1)S(1)}, u32[]{:S(2)}, u32[]{:S(2)}) collective-permute-start(bf16[64,5120]{1,0:T(8,128)(2,1)S(1)} %collective-permute-done.16.refs_0_), channel_id=1, source_target_pairs={{0,4},{1,13},{2,6},{3,15},{4,8},{5,1},{6,10},{7,3},{8,12},{9,5},{1... | collective-permute-start | bytes 1966088 | tf_op jit(solution)/shard_map/ppermute | solution.py:183
  56.3 21.4 %collective-permute-start.31 = (bf16[64,5120]{1,0:T(8,128)(2,1)S(1)}, bf16[64,5120]{1,0:T(8,128)(2,1)S(1)}, u32[]{:S(2)}, u32[]{:S(2)}) collective-permute-start(bf16[64,5120]{1,0:T(8,128)(2,1)S(1)} %collective-permute-done.16.refs_0_), channel_id=1, source_target_pairs={{0,2},{1,3},{2,0},{3,1},{4,6},{5,7},{6,4},{7,5},{8,10},{9,11},{10,... | collective-permute-start | bytes 1966088 | tf_op jit(solution)/shard_map/ppermute | solution.py:183
  57.7 12.6 %slice-start.6 = ((s8[8847360]{0:T(1024)(128)(4,1)}), s8[4194304]{0:T(1024)(128)(4,1)S(1)}, s32[]{:S(2)}) async-start(s8[8847360]{0:T(1024)(128)(4,1)} %bitcast.16), calls=%async_computation.7 | async-start | bytes 8388608
  57.7 12.6 %slice-start.7 = ((s8[8847360]{0:T(1024)(128)(4,1)}), s8[4194304]{0:T(1024)(128)(4,1)S(1)}, s32[]{:S(2)}) async-start(s8[8847360]{0:T(1024)(128)(4,1)} %bitcast.16), calls=%async_computation.8 | async-start | bytes 8388608
  57.7 12.6 %slice-start.8 = ((s8[8847360]{0:T(1024)(128)(4,1)}), s8[458752]{0:T(1024)(128)(4,1)S(1)}, s32[]{:S(2)}) async-start(s8[8847360]{0:T(1024)(128)(4,1)} %bitcast.16), calls=%async_computation.9 | async-start | bytes 917504
  57.7 9.4 %collective-permute-start.22 = (bf16[32,5248]{1,0:T(8,128)(2,1)S(1)}, bf16[32,5248]{1,0:T(8,128)(2,1)S(1)}, u32[]{:S(2)}, u32[]{:S(2)}) collective-permute-start(bf16[32,5248]{1,0:T(8,128)(2,1)S(1)} %get-tuple-element.166), channel_id=1, source_target_pairs={{0,1},{1,0},{2,3},{3,2},{4,5},{5,4},{6,7},{7,6},{8,9},{9,8},{10,11... | collective-permute-start | bytes 1007624 | tf_op jit(solution)/shard_map/ppermute | solution.py:183
  66.4 1.7 %collective-permute-start.26 = (bf16[32,5248]{1,0:T(8,128)(2,1)S(1)}, bf16[32,5248]{1,0:T(8,128)(2,1)S(1)}, u32[]{:S(2)}, u32[]{:S(2)}) collective-permute-start(bf16[32,5248]{1,0:T(8,128)(2,1)S(1)} %get-tuple-element.162), channel_id=1, source_target_pairs={{0,1},{1,0},{2,3},{3,2},{4,5},{5,4},{6,7},{7,6},{8,9},{9,8},{10,11... | collective-permute-start | bytes 1007624 | tf_op jit(solution)/shard_map/ppermute | solution.py:183
  66.6 2.1 %collective-permute-start.27 = (bf16[32,5248]{1,0:T(8,128)(2,1)S(1)}, bf16[32,5248]{1,0:T(8,128)(2,1)S(1)}, u32[]{:S(2)}, u32[]{:S(2)}) collective-permute-start(bf16[32,5248]{1,0:T(8,128)(2,1)S(1)} %get-tuple-element.161), channel_id=1, source_target_pairs={{0,1},{1,0},{2,3},{3,2},{4,5},{5,4},{6,7},{7,6},{8,9},{9,8},{10,11... | collective-permute-start | bytes 1007624 | tf_op jit(solution)/shard_map/ppermute | solution.py:183
  67.1 2.0 %collective-permute-start.23 = (bf16[32,5248]{1,0:T(8,128)(2,1)S(1)}, bf16[32,5248]{1,0:T(8,128)(2,1)S(1)}, u32[]{:S(2)}, u32[]{:S(2)}) collective-permute-start(bf16[32,5248]{1,0:T(8,128)(2,1)S(1)} %get-tuple-element.165), channel_id=1, source_target_pairs={{0,1},{1,0},{2,3},{3,2},{4,5},{5,4},{6,7},{7,6},{8,9},{9,8},{10,11... | collective-permute-start | bytes 1007624 | tf_op jit(solution)/shard_map/ppermute | solution.py:183
  68.2 1.6 %collective-permute-start.24 = (bf16[32,5248]{1,0:T(8,128)(2,1)S(1)}, bf16[32,5248]{1,0:T(8,128)(2,1)S(1)}, u32[]{:S(2)}, u32[]{:S(2)}) collective-permute-start(bf16[32,5248]{1,0:T(8,128)(2,1)S(1)} %get-tuple-element.164), channel_id=1, source_target_pairs={{0,1},{1,0},{2,3},{3,2},{4,5},{5,4},{6,7},{7,6},{8,9},{9,8},{10,11... | collective-permute-start | bytes 1007624 | tf_op jit(solution)/shard_map/ppermute | solution.py:183
  68.6 1.6 %collective-permute-start.25 = (bf16[32,5248]{1,0:T(8,128)(2,1)S(1)}, bf16[32,5248]{1,0:T(8,128)(2,1)S(1)}, u32[]{:S(2)}, u32[]{:S(2)}) collective-permute-start(bf16[32,5248]{1,0:T(8,128)(2,1)S(1)} %get-tuple-element.163), channel_id=1, source_target_pairs={{0,1},{1,0},{2,3},{3,2},{4,5},{5,4},{6,7},{7,6},{8,9},{9,8},{10,11... | collective-permute-start | bytes 1007624 | tf_op jit(solution)/shard_map/ppermute | solution.py:183
  69.1 23.0 %collective-permute-start.21 = (bf16[64,5248]{1,0:T(8,128)(2,1)S(1)}, bf16[64,5248]{1,0:T(8,128)(2,1)S(1)}, u32[]{:S(2)}, u32[]{:S(2)}) collective-permute-start(bf16[64,5248]{1,0:T(8,128)(2,1)S(1)} %collective-permute-done.8.refs_0_), channel_id=1, source_target_pairs={{0,4},{1,13},{2,6},{3,15},{4,8},{5,1},{6,10},{7,3},{8,12},{9,5},{1... | collective-permute-start | bytes 2015240 | tf_op jit(solution)/shard_map/ppermute | solution.py:183
  77.7 16.9 %collective-permute-start.39 = (bf16[64,5120]{1,0:T(8,128)(2,1)S(1)}, bf16[64,5120]{1,0:T(8,128)(2,1)S(1)}, u32[]{:S(2)}, u32[]{:S(2)}) collective-permute-start(bf16[64,5120]{1,0:T(8,128)(2,1)S(1)} %collective-permute-done.30.refs_3_), channel_id=1, source_target_pairs={{0,2},{1,3},{2,0},{3,1},{4,6},{5,7},{6,4},{7,5},{8,10},{9,11},{10,... | collective-permute-start | bytes 1966088 | tf_op jit(solution)/shard_map/ppermute | solution.py:183
  79.5 1.6 %collective-permute-start.32 = (bf16[32,5120]{1,0:T(8,128)(2,1)S(1)}, bf16[32,5120]{1,0:T(8,128)(2,1)S(1)}, u32[]{:S(2)}, u32[]{:S(2)}) collective-permute-start(bf16[32,5120]{1,0:T(8,128)(2,1)S(1)} %get-tuple-element.174), channel_id=1, source_target_pairs={{0,1},{1,0},{2,3},{3,2},{4,5},{5,4},{6,7},{7,6},{8,9},{9,8},{10,11... | collective-permute-start | bytes 983048 | tf_op jit(solution)/shard_map/ppermute | solution.py:183
  79.5 2.1 %collective-permute-start.33 = (bf16[32,5120]{1,0:T(8,128)(2,1)S(1)}, bf16[32,5120]{1,0:T(8,128)(2,1)S(1)}, u32[]{:S(2)}, u32[]{:S(2)}) collective-permute-start(bf16[32,5120]{1,0:T(8,128)(2,1)S(1)} %get-tuple-element.173), channel_id=1, source_target_pairs={{0,1},{1,0},{2,3},{3,2},{4,5},{5,4},{6,7},{7,6},{8,9},{9,8},{10,11... | collective-permute-start | bytes 983048 | tf_op jit(solution)/shard_map/ppermute | solution.py:183
  80.1 2.0 %collective-permute-start.34 = (bf16[32,5120]{1,0:T(8,128)(2,1)S(1)}, bf16[32,5120]{1,0:T(8,128)(2,1)S(1)}, u32[]{:S(2)}, u32[]{:S(2)}) collective-permute-start(bf16[32,5120]{1,0:T(8,128)(2,1)S(1)} %get-tuple-element.172), channel_id=1, source_target_pairs={{0,1},{1,0},{2,3},{3,2},{4,5},{5,4},{6,7},{7,6},{8,9},{9,8},{10,11... | collective-permute-start | bytes 983048 | tf_op jit(solution)/shard_map/ppermute | solution.py:183
  81.2 1.6 %collective-permute-start.35 = (bf16[32,5120]{1,0:T(8,128)(2,1)S(1)}, bf16[32,5120]{1,0:T(8,128)(2,1)S(1)}, u32[]{:S(2)}, u32[]{:S(2)}) collective-permute-start(bf16[32,5120]{1,0:T(8,128)(2,1)S(1)} %get-tuple-element.171), channel_id=1, source_target_pairs={{0,1},{1,0},{2,3},{3,2},{4,5},{5,4},{6,7},{7,6},{8,9},{9,8},{10,11... | collective-permute-start | bytes 983048 | tf_op jit(solution)/shard_map/ppermute | solution.py:183
  81.6 1.6 %collective-permute-start.28 = (bf16[32,5120]{1,0:T(8,128)(2,1)S(1)}, bf16[32,5120]{1,0:T(8,128)(2,1)S(1)}, u32[]{:S(2)}, u32[]{:S(2)}) collective-permute-start(bf16[32,5120]{1,0:T(8,128)(2,1)S(1)} %get-tuple-element.176), channel_id=1, source_target_pairs={{0,1},{1,0},{2,3},{3,2},{4,5},{5,4},{6,7},{7,6},{8,9},{9,8},{10,11... | collective-permute-start | bytes 983048 | tf_op jit(solution)/shard_map/ppermute | solution.py:183
  82.1 1.6 %collective-permute-start.29 = (bf16[32,5120]{1,0:T(8,128)(2,1)S(1)}, bf16[32,5120]{1,0:T(8,128)(2,1)S(1)}, u32[]{:S(2)}, u32[]{:S(2)}) collective-permute-start(bf16[32,5120]{1,0:T(8,128)(2,1)S(1)} %get-tuple-element.175), channel_id=1, source_target_pairs={{0,1},{1,0},{2,3},{3,2},{4,5},{5,4},{6,7},{7,6},{8,9},{9,8},{10,11... | collective-permute-start | bytes 983048 | tf_op jit(solution)/shard_map/ppermute | solution.py:183
  82.8 26.0 %collective-permute-start.20 = (bf16[64,5248]{1,0:T(8,128)(2,1)S(1)}, bf16[64,5248]{1,0:T(8,128)(2,1)S(1)}, u32[]{:S(2)}, u32[]{:S(2)}) collective-permute-start(bf16[64,5248]{1,0:T(8,128)(2,1)S(1)} %collective-permute-done.9.refs_3_), channel_id=1, source_target_pairs={{0,4},{1,13},{2,6},{3,15},{4,8},{5,1},{6,10},{7,3},{8,12},{9,5},{1... | collective-permute-start | bytes 2015240 | tf_op jit(solution)/shard_map/ppermute | solution.py:183
  92.1 16.9 %collective-permute-start.36 = (bf16[64,5248]{1,0:T(8,128)(2,1)S(1)}, bf16[64,5248]{1,0:T(8,128)(2,1)S(1)}, u32[]{:S(2)}, u32[]{:S(2)}) collective-permute-start(bf16[64,5248]{1,0:T(8,128)(2,1)S(1)} %collective-permute-done.21.refs_3_), channel_id=1, source_target_pairs={{0,2},{1,3},{2,0},{3,1},{4,6},{5,7},{6,4},{7,5},{8,10},{9,11},{10,... | collective-permute-start | bytes 2015240 | tf_op jit(solution)/shard_map/ppermute | solution.py:183
  94.6 7.6 %collective-permute-start.40 = (bf16[64,5120]{1,0:T(8,128)(2,1)S(1)}, bf16[64,5120]{1,0:T(8,128)(2,1)S(1)}, u32[]{:S(2)}, u32[]{:S(2)}) collective-permute-start(bf16[64,5120]{1,0:T(8,128)(2,1)S(1)} %collective-permute-done.39.refs_3_), channel_id=1, source_target_pairs={{0,1},{1,0},{2,3},{3,2},{4,5},{5,4},{6,7},{7,6},{8,9},{9,8},{10,11... | collective-permute-start | bytes 1966088 | tf_op jit(solution)/shard_map/ppermute | solution.py:183
  94.6 2.5 %collective-permute-start.37 = (bf16[32,5248]{1,0:T(8,128)(2,1)S(1)}, bf16[32,5248]{1,0:T(8,128)(2,1)S(1)}, u32[]{:S(2)}, u32[]{:S(2)}) collective-permute-start(bf16[32,5248]{1,0:T(8,128)(2,1)S(1)} %get-tuple-element.160), channel_id=1, source_target_pairs={{0,1},{1,0},{2,3},{3,2},{4,5},{5,4},{6,7},{7,6},{8,9},{9,8},{10,11... | collective-permute-start | bytes 1007624 | tf_op jit(solution)/shard_map/ppermute | solution.py:183
  95.2 2.4 %collective-permute-start.38 = (bf16[32,5248]{1,0:T(8,128)(2,1)S(1)}, bf16[32,5248]{1,0:T(8,128)(2,1)S(1)}, u32[]{:S(2)}, u32[]{:S(2)}) collective-permute-start(bf16[32,5248]{1,0:T(8,128)(2,1)S(1)} %get-tuple-element.159), channel_id=1, source_target_pairs={{0,1},{1,0},{2,3},{3,2},{4,5},{5,4},{6,7},{7,6},{8,9},{9,8},{10,11... | collective-permute-start | bytes 1007624 | tf_op jit(solution)/shard_map/ppermute | solution.py:183
  109.0 2.1 %collective-permute-start.41 = (bf16[64,5248]{1,0:T(8,128)(2,1)S(1)}, bf16[64,5248]{1,0:T(8,128)(2,1)S(1)}, u32[]{:S(2)}, u32[]{:S(2)}) collective-permute-start(bf16[64,5248]{1,0:T(8,128)(2,1)S(1)} %collective-permute-done.20.refs_0_), channel_id=1, source_target_pairs={{0,1},{1,0},{2,3},{3,2},{4,5},{5,4},{6,7},{7,6},{8,9},{9,8},{10,11... | collective-permute-start | bytes 2015240 | tf_op jit(solution)/shard_map/ppermute | solution.py:183
  109.1 3.0 %collective-permute-start.42 = (bf16[64,5248]{1,0:T(8,128)(2,1)S(1)}, bf16[64,5248]{1,0:T(8,128)(2,1)S(1)}, u32[]{:S(2)}, u32[]{:S(2)}) collective-permute-start(bf16[64,5248]{1,0:T(8,128)(2,1)S(1)} %collective-permute-done.36.refs_2_), channel_id=1, source_target_pairs={{0,1},{1,0},{2,3},{3,2},{4,5},{5,4},{6,7},{7,6},{8,9},{9,8},{10,11... | collective-permute-start | bytes 2015240 | tf_op jit(solution)/shard_map/ppermute | solution.py:183
  116.9 1.4 %collective-permute-start.43 = (bf16[128,512]{1,0:T(8,128)(2,1)S(1)}, bf16[128,512]{1,0:T(8,128)(2,1)S(1)}, u32[]{:S(2)}, u32[]{:S(2)}) collective-permute-start(bf16[128,512]{1,0:T(8,128)(2,1)S(1)} %slice.15), channel_id=1, source_target_pairs={{0,1},{1,0},{2,3},{3,2},{4,5},{5,4},{6,7},{7,6},{8,9},{9,8},{10,11... | collective-permute-start | bytes 393224 | tf_op jit(solution)/shard_map/ppermute | solution.py:183
